TPU v7x, 128 devices: a whole 4x4x4 slice. The times are simulated.
128 devices in a mesh: sub: 32 (over x, z, core), row: 4 (over y).
Axes of the slice: x: 4, y: 4, z: 4, core: 2. Of those that a mesh axis runs over, the one named last changes fastest.
Arguments:
- forces: float32 [64, 16, 2600], P('sub', None, 'row'), may hold values from -16 to 16
- inverse_h: bfloat16 [64, 2600, 2600], P('sub', 'row'), may hold values from -2 to 12, as said below
- schur_matrix: bfloat16 [64, 2600, 2600], P('sub', 'row'), may hold values from -2 to 12, as said below
- coarse_inv: float32 [1024, 1024], P(('sub', 'row')), may hold values from -1 to 4, as said below
- face_perm: int32 [64, 6, 384], P('sub', None, 'row'), may hold values from 0 to 95, as said below
- corner_rows: int32 [64, 24], P('sub'), may hold values from 576 to 2599, as said below
- corner_ids: int32 [64, 24], P('sub'), may hold values from 0 to 1023
- corner_count: int32 [64], P('sub'), may hold values from 8 to 24, as said below
Outputs:
- multipliers: float32 [64, 16, 2600], P('sub', None, 'row')
- residual: float32 [64, 16, 2600], P('sub', None, 'row')
Inputs may be any that keep to these rules, and one draw needn't show every extreme that they name: `inverse_h`: for each subdomain the matrix is symmetric positive definite. `schur_matrix`: for each subdomain the matrix is symmetric positive definite. `coarse_inv`: the matrix is symmetric positive definite. For each subdomain s, face f and block q, entries q * 96 to q * 96 + 95 of face_perm[s, f] are a permutation of 0 to 95, and the same entries of face_perm[partner(s, f), f XOR 1] hold its inverse. `corner_rows`: the 24 rows of a subdomain are distinct and none of them is a face row. `corner_count`: some subdomain has all 24 slots live.
All inputs are finite; a program needn't handle non-finite values.
Results may differ from a plain program's by a relative error of at most 0.009.
The roundings to bfloat16 on the way count: a program that leaves them out, or rounds other values in their place, can miss the bound.
Values may be sent and summed in bfloat16 or wider, within the bound.
A program may use at most 128 MiB of HBM per device.

v0:
```python
import jax
import jax.numpy as jnp
from jax import lax
from jax.sharding import PartitionSpec as P

ITERS = 2


HIGHEST = lax.Precision.HIGHEST


def partner(block, axis, distance):
    count = lax.axis_size(axis)
    route = []
    for low in range(count):
        high = low | 1 << distance
        if high != low and high < count:
            route += [(low, high), (high, low)]
    return lax.ppermute(block, axis, route)


def from_behind(value, axis, steps):
    count = lax.axis_size(axis)
    leading, last = (max(0, -steps), min(count, count - steps))
    return lax.ppermute(value, axis, [(source, source + steps) for source in range(leading, last)])


def passed_along(block, axis, distance):
    devices = range(lax.axis_size(axis))
    route = [((i - distance) % len(devices), i) for i in devices]
    return lax.ppermute(block, axis, route)


def block_product(vectors, matrices):
    rounded = vectors.astype(jnp.bfloat16)
    partial_terms = jnp.einsum(
        "srb,sbk->srk", rounded, matrices, preferred_element_type=jnp.float32
    )
    return lax.psum_scatter(partial_terms, "row", scatter_dimension=2, tiled=True)


def face_jump(values, face_perm):
    sub_count = lax.axis_size("sub")
    log_sub = sub_count.bit_length() - 1
    span_y = 2 ** ((log_sub - 1) // 2)
    step_y = 2
    step_z = 2 * span_y
    slot_total, case_count, block_len = values.shape
    face_count, face_rows = (face_perm.shape[1], face_perm.shape[2])
    face_part = values[:, :, : face_count * face_rows].reshape(
        slot_total, case_count, face_count, face_rows
    )
    faces_of = [face_part[:, :, face_id, :] for face_id in range(face_count)]
    remote_all = [None] * face_count
    for face_id in (0, 1):
        edge_piece = faces_of[1][slot_total - 1 :] if face_id == 0 else faces_of[0][:1]
        across = partner(edge_piece, "sub", 0)
        if face_id == 0:
            remote_all[0] = jnp.concatenate([across, faces_of[1][: slot_total - 1]], axis=0)
        else:
            remote_all[1] = jnp.concatenate([faces_of[0][1:], across], axis=0)
    grid_y = lax.axis_index("sub") // 2 % span_y
    for face_id, sign in ((2, 1), (3, -1)):
        sent = faces_of[face_id ^ 1]
        send_edge = span_y - 1 if sign == 1 else 0
        at_edge = grid_y == send_edge
        near_part = jnp.where(at_edge, jnp.zeros_like(sent), sent)
        far_part = jnp.where(at_edge, sent, jnp.zeros_like(sent))
        near = from_behind(near_part, "sub", sign * step_y)
        far = from_behind(far_part, "sub", -sign * step_y * (span_y - 1))
        remote_all[face_id] = near + far
    for face_id, sign in ((4, 1), (5, -1)):
        remote_all[face_id] = passed_along(faces_of[face_id ^ 1], "sub", sign * step_z)
    remote_stack = jnp.stack(remote_all, axis=2)
    perm_hot = (face_perm[:, :, :, None] == jnp.arange(face_rows)[None, None, None, :]).astype(
        jnp.float32
    )
    picked = jnp.einsum("tlfj,tfij->tlfi", remote_stack, perm_hot, precision=HIGHEST)
    stacked = (face_part - picked).reshape(slot_total, case_count, face_count * face_rows)
    filler = jnp.zeros((slot_total, case_count, block_len - face_count * face_rows), jnp.float32)
    return jnp.concatenate([stacked, filler], axis=2)


def coarse_term(flex, matrices, coarse_inv, corner_rows, corner_ids, corner_count):
    slot_total, case_count, block_len = flex.shape
    slot_count = corner_rows.shape[1]
    full_rows = matrices.shape[2]
    first_row = lax.axis_index("row") * block_len
    live_mask = (jnp.arange(slot_count)[None, :] < corner_count[:, None]).astype(jnp.float32)
    local_rows = corner_rows - first_row
    pick_rows = (jnp.arange(block_len)[None, :, None] == local_rows[:, None, :]).astype(
        jnp.float32
    ) * live_mask[:, None, :]
    at_corner = jnp.einsum("srb,sbl->srl", flex, pick_rows, precision=HIGHEST)
    coarse_count = coarse_inv.shape[1]
    coarse_pick = (corner_ids[:, :, None] == jnp.arange(coarse_count)[None, None, :]).astype(
        jnp.float32
    ) * live_mask[:, :, None]
    contrib = jnp.einsum("srl,slc->rc", at_corner, coarse_pick, precision=HIGHEST)
    owned_part = lax.psum_scatter(contrib, ("sub", "row"), scatter_dimension=1, tiled=True)
    partial_coarse = jnp.dot(owned_part, coarse_inv, precision=HIGHEST)
    coarse = lax.psum(partial_coarse, ("sub", "row"))
    spread = jnp.einsum("rc,slc->srl", coarse, coarse_pick, precision=HIGHEST).astype(jnp.bfloat16)
    column_hot = (jnp.arange(full_rows)[None, :, None] == corner_rows[:, None, :]).astype(
        jnp.bfloat16
    )
    h_cols = jnp.einsum(
        "sbk,skl->sbl", matrices, column_hot, preferred_element_type=jnp.float32
    ).astype(jnp.bfloat16)
    return flex + jnp.einsum("srl,sbl->srb", spread, h_cols, preferred_element_type=jnp.float32)


def inner_products(left, right):
    return lax.psum(jnp.einsum("sik,sjk->ij", left, right, precision=HIGHEST), ("sub", "row"))


def combine(vectors, coeffs):
    return jnp.einsum("sjk,ji->sik", vectors, coeffs, precision=HIGHEST)


def chol_solve(matrix, rhs_matrix):
    factor = jnp.linalg.cholesky(matrix)
    return jax.scipy.linalg.cho_solve((factor, True), rhs_matrix)


def body(
    forces, inverse_h, schur_matrix, coarse_inv, face_perm, corner_rows, corner_ids, corner_count
):

    def dual(vectors):
        flex = block_product(vectors, inverse_h)
        applied = coarse_term(flex, inverse_h, coarse_inv, corner_rows, corner_ids, corner_count)
        return face_jump(applied, face_perm)

    def precond(vectors):
        return face_jump(block_product(vectors, schur_matrix), face_perm)

    residual = dual(forces)
    multipliers = jnp.zeros_like(residual)
    zvec = precond(residual)
    direction = zvec
    energy = inner_products(residual, zvec)
    for iteration in range(ITERS):
        image_vec = dual(direction)
        curvature = inner_products(direction, image_vec)
        step_size = chol_solve(curvature, energy)
        multipliers = multipliers + combine(direction, step_size)
        residual = residual - combine(image_vec, step_size)
        if iteration + 1 < ITERS:
            zvec = precond(residual)
            energy_next = inner_products(residual, zvec)
            blend = chol_solve(energy, energy_next)
            direction = zvec + combine(direction, blend)
            energy = energy_next
    return (multipliers, residual)


def solution(mesh):
    in_specs = (
        P("sub", None, "row"),
        P("sub", "row", None),
        P("sub", "row", None),
        P(("sub", "row"), None),
        P("sub", None, "row"),
        P("sub", None),
        P("sub", None),
        P("sub"),
    )
    out_specs = (P("sub", None, "row"), P("sub", None, "row"))
    return jax.shard_map(body, mesh=mesh, in_specs=in_specs, out_specs=out_specs, check_vma=False)
```

profile of v0, /device:TPU:1, one launch (start us, length us, event | category | flops | bytes accessed | tf_op | source)
XLA Modules:
  0.0 1417.6 jit_solution(13709198360221137226)
XLA Ops:
  7.3 4.8 fusion.10
  13.5 41.9 %all-reduce.32.cloned.1.call-done = f32[2,16,2600]{2,1,0:T(8,128)} async-done(((f32[2,16,2600]{2,1,0:T(8,128)}), f32[2,16,2600]{2,1,0:T(8,128)}) %all-reduce.32.cloned.1.call-update) | async-done | bytes 332816
  57.7 143.3 %all-reduce.34.cloned.1.call-done = f32[16,1024]{1,0:T(8,128)} async-done(((f32[16,1024]{1,0:T(8,128)}), f32[16,1024]{1,0:T(8,128)}) %all-reduce.34.cloned.1.call-update) | async-done | bytes 65552
  201.0 1.6 fusion.100
  202.7 5.0 fusion.12
  207.7 134.0 %all-reduce.26.cloned.1.call-done = f32[16,1024]{1,0:T(8,128)} async-done(((f32[16,1024]{1,0:T(8,128)}), f32[16,1024]{1,0:T(8,128)}) %all-reduce.26.cloned.1.call-update) | async-done | bytes 65552 | tf_op jit(solution)/shard_map/psum | solution.py:102
  341.7 1.5 convolution_convert_fusion.2
  344.6 1.3 collective-permute-start.4
  345.9 4.9 collective-permute-start.5
  350.9 3.2 collective-permute-start.2
  354.1 1.3 collective-permute-start.3
  357.0 1.8 collective-permute-start.6
  359.9 1.3 collective-permute-done.6
  362.6 4.8 fusion.2
  367.4 41.0 %all-reduce.36.cloned.1.call-done = f32[2,16,2600]{2,1,0:T(8,128)} async-done(((f32[2,16,2600]{2,1,0:T(8,128)}), f32[2,16,2600]{2,1,0:T(8,128)}) %all-reduce.36.cloned.1.call-update) | async-done | bytes 332816
  409.7 1.3 collective-permute-start.12
  411.0 5.7 collective-permute-start.13
  416.6 3.4 collective-permute-start.8
  420.1 3.8 collective-permute-start.10
  423.9 1.3 collective-permute-start.11
  426.4 1.8 collective-permute-start.14
  428.3 1.6 collective-permute-start.15
  432.0 4.8 fusion.6
  436.9 41.2 %all-reduce.38.cloned.1.call-done = f32[2,16,2600]{2,1,0:T(8,128)} async-done(((f32[2,16,2600]{2,1,0:T(8,128)}), f32[2,16,2600]{2,1,0:T(8,128)}) %all-reduce.38.cloned.1.call-update) | async-done | bytes 332816
  480.3 143.2 %all-reduce.40.cloned.1.call-done = f32[16,1024]{1,0:T(8,128)} async-done(((f32[16,1024]{1,0:T(8,128)}), f32[16,1024]{1,0:T(8,128)}) %all-reduce.40.cloned.1.call-update) | async-done | bytes 65552
  623.5 1.6 fusion.98
  625.4 138.8 %all-reduce.28.cloned.1.call-done = f32[16,1024]{1,0:T(8,128)} async-done(((f32[16,1024]{1,0:T(8,128)}), f32[16,1024]{1,0:T(8,128)}) %all-reduce.28.cloned.1.call-update) | async-done | bytes 65552 | tf_op jit(solution)/shard_map/psum | solution.py:102
  764.2 1.5 convolution_convert_fusion.1
  767.1 1.3 collective-permute-start.20
  768.4 4.9 collective-permute-start.21
  773.4 3.2 collective-permute-start.18
  776.6 1.3 collective-permute-start.19
  779.6 1.8 collective-permute-start.22
  782.4 1.3 collective-permute-done.22
  785.3 66.3 %all-reduce.13 = (f32[16,16]{0,1:T(8,128)S(1)}, f32[16,16]{0,1:T(8,128)S(1)}) all-reduce(f32[16,16]{0,1:T(8,128)S(1)} %convolution_bitcast_fusion.16, f32[16,16]{0,1:T(8,128)S(1)} %convolution_bitcast_fusion.17), channel_id=1, replica_groups=mesh['sub'=32,'row'=4] {'sub','row'}, use_global_device_ids=true, to_apply=%region_10.12 | all-reduce | flops 512 | bytes 4096 | tf_op jit(solution)/shard_map/psum | solution.py:114
  851.8 1.5 cholesky.70
  853.3 1.5 cholesky.59
  856.1 1.2 custom-call.9
  857.9 4.8 fusion
  864.1 1.2 custom-call.10
  865.3 34.0 %all-reduce.42.cloned.1.call-done = f32[2,16,2600]{2,1,0:T(8,128)} async-done(((f32[2,16,2600]{2,1,0:T(8,128)}), f32[2,16,2600]{2,1,0:T(8,128)}) %all-reduce.42.cloned.1.call-update) | async-done | bytes 332816
  900.5 1.3 collective-permute-start.28
  901.8 5.7 collective-permute-start.29
  907.5 3.4 collective-permute-start.24
  910.9 3.8 collective-permute-start.26
  914.7 1.3 collective-permute-start.27
  917.3 1.8 collective-permute-start.30
  919.1 1.6 collective-permute-start.31
  923.1 65.8 %psum.53 = f32[16,16]{1,0:T(8,128)S(1)} all-reduce(f32[16,16]{1,0:T(8,128)S(1)} %convolution_bitcast_fusion.14), channel_id=1, replica_groups=mesh['sub'=32,'row'=4] {'sub','row'}, use_global_device_ids=true, to_apply=%region_12.15 | all-reduce | flops 256 | bytes 2048 | tf_op jit(solution)/shard_map/psum | solution.py:114
  989.5 4.8 fusion.4
  994.4 37.0 %all-reduce.44.cloned.1.call-done = f32[2,16,2600]{2,1,0:T(8,128)} async-done(((f32[2,16,2600]{2,1,0:T(8,128)}), f32[2,16,2600]{2,1,0:T(8,128)}) %all-reduce.44.cloned.1.call-update) | async-done | bytes 332816
  1033.6 143.1 %all-reduce.46.cloned.1.call-done = f32[16,1024]{1,0:T(8,128)} async-done(((f32[16,1024]{1,0:T(8,128)}), f32[16,1024]{1,0:T(8,128)}) %all-reduce.46.cloned.1.call-update) | async-done | bytes 65552
  1176.8 1.6 fusion.96
  1178.6 138.9 %all-reduce.30.cloned.1.call-done = f32[16,1024]{1,0:T(8,128)} async-done(((f32[16,1024]{1,0:T(8,128)}), f32[16,1024]{1,0:T(8,128)}) %all-reduce.30.cloned.1.call-update) | async-done | bytes 65552 | tf_op jit(solution)/shard_map/psum | solution.py:102
  1317.5 1.5 convolution_convert_fusion
  1320.3 1.3 collective-permute-start.36
  1321.6 4.9 collective-permute-start.37
  1326.6 3.2 collective-permute-start.34
  1329.8 1.3 collective-permute-start.35
  1332.8 1.8 collective-permute-start.38
  1335.6 1.3 collective-permute-done.38
  1338.6 66.2 %psum.55 = f32[16,16]{0,1:T(8,128)S(1)} all-reduce(f32[16,16]{0,1:T(8,128)S(1)} %convolution_bitcast_fusion.12), channel_id=1, replica_groups=mesh['sub'=32,'row'=4] {'sub','row'}, use_global_device_ids=true, to_apply=%region_16.19 | all-reduce | flops 256 | bytes 2048 | tf_op jit(solution)/shard_map/psum | solution.py:114
  1404.9 1.5 cholesky.81
  1407.7 1.2 custom-call.11
  (204 shorter events, 41.9 us)
Async XLA Ops:
  7.2 193.8 %copy-start = (f32[8,1024]{1,0:T(8,128)S(1)}, f32[8,1024]{1,0:T(8,128)}, u32[]{:S(2)}) copy-start(f32[8,1024]{1,0:T(8,128)} %param.14) | copy-start | bytes 98308
  7.2 5.1 copy-start.5
  7.2 5.0 copy-start.4
  7.2 6.3 copy-start.2
  7.2 49.5 %copy-start.3 = (s32[2,24]{1,0:T(2,128)S(1)}, s32[2,24]{1,0:T(2,128)}, u32[]{:S(2)}) copy-start(s32[2,24]{1,0:T(2,128)} %param.17) | copy-start | bytes 580
  7.2 200.4 %copy-start.1 = (s32[2,6,96]{2,0,1:T(2,128)S(1)}, s32[2,6,96]{2,0,1:T(2,128)}, u32[]{:S(2)}) copy-start(s32[2,6,96]{2,0,1:T(2,128)} %param.15) | copy-start | bytes 13828
  7.2 48.2 %all-reduce.32.cloned.1.call-start = ((), (), s32[]{:S(2)}) async-start(), calls=%async_computation.3 | async-start | bytes 688128
  12.1 188.9 %all-reduce.34.cloned.1.call-start = ((), (), s32[]{:S(2)}) async-start(), calls=%async_computation.4 | async-start | bytes 131072
  57.6 284.1 %all-reduce.26.cloned.1.call-start = ((), (), s32[]{:S(2)}) async-start(), calls=%async_computation | async-start | bytes 131072 | tf_op jit(solution)/shard_map/psum | solution.py:102
  202.6 205.9 %all-reduce.36.cloned.1.call-start = ((), (), s32[]{:S(2)}) async-start(), calls=%async_computation.5 | async-start | bytes 688128
  344.6 15.3 %collective-permute-start.4 = (f32[2,16,96]{2,1,0:T(8,128)S(1)}, f32[2,16,96]{2,1,0:T(8,128)S(1)}, u32[]{:S(2)}, u32[]{:S(2)}) collective-permute-start(f32[2,16,96]{2,1,0:T(8,128)S(1)} %get-tuple-element.63), channel_id=1, source_target_pairs={{8,0},{12,4},{16,8},{20,12},{24,16},{28,20},{32,24},{36,28},{40,32... | collective-permute-start | bytes 36872 | tf_op jit(solution)/shard_map/ppermute | solution.py:25
  345.9 14.0 collective-permute-start.5
  350.8 4.6 collective-permute-start
  350.9 8.0 collective-permute-start.2
  354.1 5.7 collective-permute-start.3
  355.4 1.7 collective-permute-start.1
  357.0 4.1 collective-permute-start.6
  358.9 2.9 collective-permute-start.7
  367.4 110.7 %all-reduce.38.cloned.1.call-start = ((), (), s32[]{:S(2)}) async-start(), calls=%async_computation.6 | async-start | bytes 688128
  409.7 20.2 %collective-permute-start.12 = (f32[2,16,96]{2,1,0:T(8,128)S(1)}, f32[2,16,96]{2,1,0:T(8,128)S(1)}, u32[]{:S(2)}, u32[]{:S(2)}) collective-permute-start(f32[2,16,96]{2,1,0:T(8,128)S(1)} %get-tuple-element.59), channel_id=1, source_target_pairs={{8,0},{12,4},{16,8},{20,12},{24,16},{28,20},{32,24},{36,28},{40,32... | collective-permute-start | bytes 36872 | tf_op jit(solution)/shard_map/ppermute | solution.py:25
  411.0 18.9 %collective-permute-start.13 = (f32[2,16,96]{2,1,0:T(8,128)S(1)}, f32[2,16,96]{2,1,0:T(8,128)S(1)}, u32[]{:S(2)}, u32[]{:S(2)}) collective-permute-start(f32[2,16,96]{2,1,0:T(8,128)S(1)} %get-tuple-element.58), channel_id=1, source_target_pairs={{0,24},{4,28},{8,32},{12,36},{16,40},{20,44},{24,48},{28,52},{32,5... | collective-permute-start | bytes 36872 | tf_op jit(solution)/shard_map/ppermute | solution.py:25
  416.6 8.5 collective-permute-start.8
  420.1 8.2 collective-permute-start.10
  423.9 6.0 collective-permute-start.11
  425.2 1.3 collective-permute-start.9
  426.4 4.5 collective-permute-start.14
  428.3 2.9 collective-permute-start.15
  436.9 186.6 %all-reduce.40.cloned.1.call-start = ((), (), s32[]{:S(2)}) async-start(), calls=%async_computation.7 | async-start | bytes 131072
  480.3 284.0 %all-reduce.28.cloned.1.call-start = ((), (), s32[]{:S(2)}) async-start(), calls=%async_computation.1 | async-start | bytes 131072 | tf_op jit(solution)/shard_map/psum | solution.py:102
  625.1 274.2 %all-reduce.42.cloned.1.call-start = ((), (), s32[]{:S(2)}) async-start(), calls=%async_computation.8 | async-start | bytes 688128
  767.1 15.3 %collective-permute-start.20 = (f32[2,16,96]{2,1,0:T(8,128)S(1)}, f32[2,16,96]{2,1,0:T(8,128)S(1)}, u32[]{:S(2)}, u32[]{:S(2)}) collective-permute-start(f32[2,16,96]{2,1,0:T(8,128)S(1)} %get-tuple-element.55), channel_id=1, source_target_pairs={{8,0},{12,4},{16,8},{20,12},{24,16},{28,20},{32,24},{36,28},{40,32... | collective-permute-start | bytes 36872 | tf_op jit(solution)/shard_map/ppermute | solution.py:25
  768.4 14.0 collective-permute-start.21
  773.3 4.6 collective-permute-start.16
  773.4 8.0 collective-permute-start.18
  776.6 5.7 collective-permute-start.19
  777.9 1.7 collective-permute-start.17
  779.6 4.1 collective-permute-start.22
  781.4 2.9 collective-permute-start.23
  862.7 168.7 %all-reduce.44.cloned.1.call-start = ((), (), s32[]{:S(2)}) async-start(), calls=%async_computation.9 | async-start | bytes 688128
  900.5 20.2 %collective-permute-start.28 = (f32[2,16,96]{2,1,0:T(8,128)S(1)}, f32[2,16,96]{2,1,0:T(8,128)S(1)}, u32[]{:S(2)}, u32[]{:S(2)}) collective-permute-start(f32[2,16,96]{2,1,0:T(8,128)S(1)} %get-tuple-element.51), channel_id=1, source_target_pairs={{8,0},{12,4},{16,8},{20,12},{24,16},{28,20},{32,24},{36,28},{40,32... | collective-permute-start | bytes 36872 | tf_op jit(solution)/shard_map/ppermute | solution.py:25
  901.8 18.9 %collective-permute-start.29 = (f32[2,16,96]{2,1,0:T(8,128)S(1)}, f32[2,16,96]{2,1,0:T(8,128)S(1)}, u32[]{:S(2)}, u32[]{:S(2)}) collective-permute-start(f32[2,16,96]{2,1,0:T(8,128)S(1)} %get-tuple-element.50), channel_id=1, source_target_pairs={{0,24},{4,28},{8,32},{12,36},{16,40},{20,44},{24,48},{28,52},{32,5... | collective-permute-start | bytes 36872 | tf_op jit(solution)/shard_map/ppermute | solution.py:25
  907.5 8.5 collective-permute-start.24
  910.9 8.2 collective-permute-start.26
  914.7 6.0 collective-permute-start.27
  916.0 1.3 collective-permute-start.25
  917.3 4.5 collective-permute-start.30
  919.1 2.9 collective-permute-start.31
  994.4 182.4 %all-reduce.46.cloned.1.call-start = ((), (), s32[]{:S(2)}) async-start(), calls=%async_computation.10 | async-start | bytes 131072
  1033.6 283.9 %all-reduce.30.cloned.1.call-start = ((), (), s32[]{:S(2)}) async-start(), calls=%async_computation.2 | async-start | bytes 131072 | tf_op jit(solution)/shard_map/psum | solution.py:102
  1320.3 15.3 %collective-permute-start.36 = (f32[2,16,96]{2,1,0:T(8,128)S(1)}, f32[2,16,96]{2,1,0:T(8,128)S(1)}, u32[]{:S(2)}, u32[]{:S(2)}) collective-permute-start(f32[2,16,96]{2,1,0:T(8,128)S(1)} %get-tuple-element.47), channel_id=1, source_target_pairs={{8,0},{12,4},{16,8},{20,12},{24,16},{28,20},{32,24},{36,28},{40,32... | collective-permute-start | bytes 36872 | tf_op jit(solution)/shard_map/ppermute | solution.py:25
  1321.6 14.0 collective-permute-start.37
  1326.5 4.6 collective-permute-start.32
  1326.6 8.0 collective-permute-start.34
  1329.8 5.8 collective-permute-start.35
  1331.2 1.7 collective-permute-start.33
  1332.8 4.1 collective-permute-start.38
  1334.6 2.9 collective-permute-start.39
Sparse Core Ops, SparseCore 0:
  12.3 43.1 all-reduce.31
  60.8 140.1 all-reduce.33
  207.0 134.6 all-reduce.25
  367.5 40.9 all-reduce.35
  437.0 41.0 all-reduce.37
  483.3 140.1 all-reduce.39
  629.5 134.6 all-reduce.27
  862.8 36.4 all-reduce.41
  994.5 36.8 all-reduce.43
  1036.6 140.1 all-reduce.45
  1182.8 134.6 all-reduce.29
where the time goes:
time: 1420 us
  waiting for transfers between devices  1050 us (74%)
  blocking collectives  198 us (14%)
  starting transfers between devices  82.1 us (6%)
  matrix products  52.7 us (4%)
  between operations  15.4 us (1%)
  other arithmetic  15.2 us (1%)
    unnamed x19, waiting for transfers between devices  625 us
    psum x3, waiting for transfers between devices, coarse_term(): coarse = lax.psum(partial_coarse, ('sub', 'row'))  412 us
    psum x3, blocking collectives, inner_products(): lax.psum(jnp.einsum('sik,sjk->ij', left, right, precision=HIGHEST), ('sub...  198 us
    ppermute x20, starting transfers between devices, from_behind(): lax.ppermute(value, axis, [(source, source + steps) for source in range(l...  56.1 us
  transfers between devices with their start and end apart: 51, of which 26 were waited for; matrix products, arithmetic and copies ran while one was open for 1% of the time, Pallas kernels for 0%

commit v1 on v0

v1 whole, which is shorter than its diff:
```python
import functools

import jax
import jax.numpy as jnp
from jax import lax
from jax.experimental import pallas as pl
from jax.experimental.pallas import tpu as pltpu
from jax.sharding import PartitionSpec as P

MESH = pl.DeviceIdType.MESH
HIGHEST = lax.Precision.HIGHEST
F32 = jnp.float32
BF16 = jnp.bfloat16

NSUB = 32
NROW = 4
LOADS = 16
FACES = 6
FACEQ = 96
WIDE = FACES * 128
BLOCK = 650
NS = 2600
KMAIN = 2560
KFULL = 2688
PART = 640
SPILL = 768
SLOTS = 48

IDS, FORCES, TPART, CFULL, HCORN, XG, CORN, JUMP, ARA, ARB = 0, 1, 2, 3, 4, 5, 9, 12, 17, 21
NSEM = 25


def lanes(shape):
    return lax.broadcasted_iota(jnp.int32, shape, 1)


def dot_nt(a, b, precision=None):
    return lax.dot_general(
        a, b, (((1,), (1,)), ((), ())), precision=precision, preferred_element_type=F32
    )


def dot_nn(a, b, precision=None):
    return lax.dot_general(
        a, b, (((1,), (0,)), ((), ())), precision=precision, preferred_element_type=F32
    )


def dot_tn(a, b, precision=None):
    return lax.dot_general(
        a, b, (((0,), (0,)), ((), ())), precision=precision, preferred_element_type=F32
    )


def lane_gather(x, idx):
    dims = lax.GatherDimensionNumbers(
        offset_dims=(),
        collapsed_slice_dims=(1,),
        start_index_map=(1,),
        operand_batching_dims=(0,),
        start_indices_batching_dims=(0,),
    )
    return lax.gather(
        x, idx[..., None], dims, (1, 1), mode=lax.GatherScatterMode.PROMISE_IN_BOUNDS
    )


def pack_tiles(pieces, shift, count):
    rows = pieces[0].shape[0]
    lane = lanes((rows, 128))
    tiles = [jnp.zeros((rows, 128), F32) for _ in range(count)]
    for f, piece in enumerate(pieces):
        a, b0 = divmod(FACEQ * f, 128)
        b = shift + b0
        if isinstance(b, int) and b == 0:
            rolled = piece
        else:
            rolled = pltpu.roll(piece, b, 1)
        if b0 == 0:
            tiles[a] = tiles[a] + rolled
        else:
            tiles[a] = tiles[a] + jnp.where(lane >= b, rolled, 0.0)
            if a + 1 < count:
                tiles[a + 1] = tiles[a + 1] + jnp.where(lane < b, rolled, 0.0)
    return tiles


def eliminate(m):
    row_id = lax.broadcasted_iota(jnp.int32, (LOADS, 128), 0)
    for k in range(LOADS):
        col = jnp.broadcast_to(m[:, k : k + 1], (LOADS, 128))
        row = jnp.broadcast_to(m[k : k + 1, :], (LOADS, 128))
        pivot = jnp.broadcast_to(col[k : k + 1, :], (LOADS, 128))
        row = row / pivot
        m = jnp.where(row_id == k, row, m - col * row)
    return pltpu.roll(m, 112, 1)


def kernel(
    forces, h_hbm, s_hbm, h_tail, c_own, perm, cr, ids, mult_out, res_out,
    hv, sv, ib, tb, ca, cat, kt, fb, xf, lhs, hco, hcb, hcf, xb, cb, sb, jb, ra, rb, gs, pidx, dv, rv, mv,
    h_sem, s_sem, send, recv,
):
    g = lax.axis_index("sub")
    q = lax.axis_index("row")
    core = lax.rem(g, 2)
    zc = lax.rem(g // 2, 4)
    xc = g // 8

    def dev(x, z, c):
        return (x * 4 + z) * 2 + c

    for f in range(FACES):
        pltpu.make_async_copy(
            h_hbm.at[:, pl.ds(FACEQ * f, FACEQ), :], hv.at[:, pl.ds(128 * f, FACEQ), :], h_sem.at[f]
        ).start()
    for f in range(FACES):
        pltpu.make_async_copy(
            s_hbm.at[:, pl.ds(FACEQ * f, FACEQ), :], sv.at[:, pl.ds(128 * f, FACEQ), :], s_sem.at[f]
        ).start()

    barrier = pltpu.get_barrier_semaphore()

    @pl.loop(1, NSUB)
    def _(k):
        pl.semaphore_signal(
            barrier, inc=1, device_id=(lax.rem(g + k, NSUB), q), device_id_type=MESH
        )

    other = g + 1 - 2 * core
    for k in range(1, NROW):
        far = lax.rem(q + k, NROW)
        pl.semaphore_signal(barrier, inc=1, device_id=(g, far), device_id_type=MESH)
        pl.semaphore_signal(barrier, inc=1, device_id=(other, far), device_id_type=MESH)

    for half in (hv, sv):
        for s in range(2):
            for f in range(FACES):
                half[s, 128 * f + FACEQ : 128 * f + 128, :] = jnp.zeros((32, NS), BF16)
    for i in range(12):
        pidx[i] = jnp.broadcast_to(perm[i : i + 1, :], (LOADS, 128))
    hco[...] = jnp.zeros((128, WIDE), BF16)
    hcf[96:128, :] = jnp.zeros((32, KFULL), BF16)
    kt[96:128, :] = jnp.zeros((32, NSUB * 128), BF16)
    gs[...] = jnp.zeros((32, 128), F32)
    for s in range(2):
        spot = jnp.broadcast_to(cr[s], (SLOTS, KFULL))
        lhs[s, LOADS:, :] = jnp.where(lanes((SLOTS, KFULL)) == spot, 1.0, 0.0).astype(BF16)

    ib[g] = ids[...]
    shift = 10 * q
    lane32 = lanes((32, 128))
    last = jnp.zeros((32, 128), F32)
    for t in range(6):
        now = pltpu.roll(forces[:, 128 * t : 128 * t + 128], shift, 1)
        fb[q, :, 128 * t : 128 * t + 128] = jnp.where(lane32 >= shift, now, last).astype(BF16)
        last = now

    pl.semaphore_wait(barrier, NSUB - 1 + 2 * (NROW - 1))

    def to_plane(src_of, dst, sem):
        @pl.loop(1, NSUB)
        def _(k):
            far = lax.rem(g + k, NSUB)
            pltpu.make_async_remote_copy(
                src_ref=src_of(far),
                dst_ref=dst,
                send_sem=send.at[sem],
                recv_sem=recv.at[sem],
                device_id=(far, q),
                device_id_type=MESH,
            ).start()

    def to_row(ref, sem):
        for k in range(1, NROW):
            pltpu.make_async_remote_copy(
                src_ref=ref,
                dst_ref=ref,
                send_sem=send.at[sem],
                recv_sem=recv.at[sem],
                device_id=(g, lax.rem(q + k, NROW)),
                device_id_type=MESH,
            ).start()

    drains = []

    def arrived(ref, sem):
        pltpu.make_async_copy(ref, ref, recv.at[sem]).wait()
        drains.append((ref, sem))

    to_plane(lambda far: ib.at[g], ib.at[g], IDS)
    to_row(fb.at[q], FORCES)

    arrived(ib.at[pl.ds(0, NSUB - 1)], IDS)

    def pick_columns(far):
        idx = ib[far]
        tile = lax.shift_right_arithmetic(idx, 7)
        lane = lax.bitwise_and(idx, 127)
        total = jnp.zeros((8, 128), F32)
        for v in range(8):
            got = lane_gather(c_own[:, 128 * v : 128 * v + 128], lane)
            total = total + jnp.where(tile == v, got, 0.0)
        return total

    ca[q, g] = pick_columns(g)

    @pl.loop(1, NSUB)
    def _(k):
        far = lax.rem(g + k, NSUB)
        tb[far] = pick_columns(far)
        pltpu.make_async_remote_copy(
            src_ref=tb.at[far],
            dst_ref=ca.at[q, g],
            send_sem=send.at[TPART],
            recv_sem=recv.at[TPART],
            device_id=(far, q),
            device_id_type=MESH,
        ).start()

    def assemble(slots, put):
        for p in range(NROW):
            first = slots[p, :, 0:128]
            if p > 0:
                first = first + slots[p - 1, :, PART:SPILL]
            put(PART * p, first)
            put(PART * p + 128, slots[p, :, 128:PART])
        put(KMAIN, slots[NROW - 1, :, PART:SPILL])

    arrived(fb.at[pl.ds(0, NROW - 1)], FORCES)

    def put_forces(start, value):
        width = value.shape[1]
        xf[:, start : start + width] = value
        lhs[0, :LOADS, start : start + width] = value[:LOADS]
        lhs[1, :LOADS, start : start + width] = value[LOADS:]

    assemble(fb, put_forces)

    for f in range(FACES):
        pltpu.make_async_copy(
            h_hbm.at[:, pl.ds(FACEQ * f, FACEQ), :], hv.at[:, pl.ds(128 * f, FACEQ), :], h_sem.at[f]
        ).wait()

    flex0 = []
    corner_h = jnp.zeros((SLOTS, WIDE), F32)
    corner_t = jnp.zeros((SLOTS, 128), F32)
    for s in range(2):
        prod = dot_nt(lhs[s, :, :KMAIN], hv[s, :, :KMAIN]) + dot_nt(
            lhs[s, :, KMAIN:NS], hv[s, :, KMAIN:NS]
        )
        tail = dot_nt(lhs[s, LOADS:, :KMAIN], h_tail[s, :, :KMAIN]) + dot_nt(
            lhs[s, LOADS:, KMAIN:NS], h_tail[s, :, KMAIN:NS]
        )
        flex0.append(prod[:LOADS])
        corner_h = corner_h + prod[LOADS:]
        corner_t = corner_t + tail
    flex0 = jnp.concatenate(flex0, axis=0)
    rv[...] = flex0
    hco[:SLOTS, :] = corner_h.astype(BF16)
    pieces = [corner_h[:, 128 * f : 128 * f + 128] for f in range(FACES)] + [corner_t]
    for t, tile in enumerate(pack_tiles(pieces, shift, 6)):
        hcb[q, :, 128 * t : 128 * t + 128] = tile.astype(BF16)
    to_row(hcb.at[q], HCORN)

    arrived(ca.at[0, pl.ds(0, NSUB - 1)], TPART)
    to_row(ca.at[q], CFULL)

    arrived(hcb.at[pl.ds(0, NROW - 1)], HCORN)

    def put_corner(start, value):
        width = value.shape[1]
        hcf[:SLOTS, start : start + width] = value
        hcf[SLOTS : 2 * SLOTS, start : start + width] = value

    assemble(hcb, put_corner)

    lane16 = lanes((LOADS, 128))
    first_sub = (lane16 < 24) | ((lane16 >= 48) & (lane16 < 72))
    own_cols = pl.ds(pl.multiple_of(128 * g, 128), 128)

    def corner_send(n, both):
        at = jnp.where(first_sub, both[:LOADS], both[LOADS:])
        high = at.astype(BF16).astype(F32)
        cb[n, :, own_cols] = jnp.where(lane16 < SLOTS, high, at - high).astype(BF16)
        to_plane(lambda far: cb.at[n, :, own_cols], cb.at[n, :, own_cols], CORN + n)

    corner_send(0, dot_nt(xf[...], hcf[...]))

    arrived(ca.at[pl.ds(0, NROW - 1)], CFULL)
    for p in range(NROW):
        for half in range(2):
            block = ca[p, 16 * half : 16 * half + 16].reshape(128, 128)
            spot = (2 * p + half) * 128
            cat[:, spot : spot + 128] = block.T[:SLOTS]

    @pl.loop(0, NSUB)
    def _(far):
        c = ib[far]
        tile = 2 * lax.bitwise_and(lax.shift_right_arithmetic(c, 3), 3) + lax.shift_right_arithmetic(c, 9)
        tile = jnp.where(c < 0, -1, tile)
        lane = 8 * lax.bitwise_and(lax.shift_right_arithmetic(c, 5), 15) + lax.bitwise_and(c, 7)
        cols = pl.ds(pl.multiple_of(128 * far, 128), 128)
        parts = []
        for a in range(SLOTS // 8):
            total = jnp.zeros((8, 128), F32)
            for v in range(8):
                got = lane_gather(cat[8 * a : 8 * a + 8, 128 * v : 128 * v + 128], lane)
                total = total + jnp.where(tile == v, got, 0.0)
            parts.append(total)
        total = jnp.concatenate(parts, axis=0)
        high = total.astype(BF16)
        kt[:SLOTS, cols] = high
        kt[SLOTS : 2 * SLOTS, cols] = (total - high.astype(F32)).astype(BF16)

    def corner_finish(n, flex):
        arrived(cb.at[n, :, pl.ds(0, (NSUB - 1) * 128)], CORN + n)
        spread = dot_nt(cb[n], kt[...])
        spread = spread + pltpu.roll(spread, 128 - SLOTS, 1)
        left = jnp.concatenate(
            [
                jnp.where(lane16 < 24, spread, 0.0),
                jnp.where((lane16 >= 24) & (lane16 < SLOTS), spread, 0.0),
            ],
            axis=0,
        ).astype(BF16)
        return flex + dot_nn(left, hco[...])

    face_targets = {
        2: dev(xc, lax.rem(zc + 3, 4), core),
        3: dev(xc, lax.rem(zc + 1, 4), core),
        4: dev(lax.rem(xc + 3, 4), zc, core),
        5: dev(lax.rem(xc + 1, 4), zc, core),
    }

    def face_of(v, t, f):
        return v[LOADS * t : LOADS * t + LOADS, 128 * f : 128 * f + 128]

    def jump_send(n, v):
        sb[n, 0] = face_of(v, 0, 0)
        sb[n, 1] = face_of(v, 1, 1)
        for f in range(2, FACES):
            for t in range(2):
                sb[n, 2 * f - 2 + t] = face_of(v, t, f)
        moves = [(0, 1, 1, other), (1, 0, 1, other)]
        moves += [(2 * f - 2, 2 * (f ^ 1) - 2, 2, face_targets[f]) for f in range(2, FACES)]
        for src, dst, size, far in moves:
            pltpu.make_async_remote_copy(
                src_ref=sb.at[n, pl.ds(src, size)],
                dst_ref=jb.at[n, pl.ds(dst, size)],
                send_sem=send.at[JUMP + n],
                recv_sem=recv.at[JUMP + n],
                device_id=(far, q),
                device_id_type=MESH,
            ).start()

    def jump_finish(n, v):
        arrived(jb.at[n], JUMP + n)
        subs = []
        for t in range(2):
            out = []
            for f in range(FACES):
                if f < 2:
                    remote = jb[n, f] if f == t else face_of(v, 1 - t, f ^ 1)
                else:
                    remote = jb[n, 2 * f - 2 + t]
                out.append(face_of(v, t, f) - lane_gather(remote, pidx[FACES * t + f]))
            subs.append(jnp.concatenate(out, axis=1))
        return jnp.concatenate(subs, axis=0)

    own_part = pl.ds(pl.multiple_of(PART * q, 128), PART)

    def gather_x(n, x):
        pieces = [x[:, 128 * f : 128 * f + 128] for f in range(FACES)]
        tiles = pack_tiles(pieces, shift, 5)
        xb[n, :, own_part] = jnp.concatenate(tiles, axis=1).astype(BF16)
        to_row(xb.at[n, :, own_part], XG + n)
        arrived(xb.at[n, :, pl.ds(0, 3 * PART)], XG + n)

    def product(n, mat):
        return jnp.concatenate(
            [dot_nt(xb[n, :LOADS, :], mat[0, :, :KMAIN]), dot_nt(xb[n, LOADS:, :], mat[1, :, :KMAIN])],
            axis=0,
        )

    chip_pos = NROW * core + q
    chip_id = g // 2

    def inner_start(n, x, y):
        total = jnp.zeros((32, 32), F32)
        for s in range(2):
            xs, ys = x[LOADS * s : LOADS * s + LOADS], y[LOADS * s : LOADS * s + LOADS]
            total = total + dot_nt(
                jnp.concatenate([xs, ys], axis=0), jnp.concatenate([ys, xs], axis=0), HIGHEST
            )
        gs[:, :32] = total
        plain = jnp.where(lane16 < LOADS, gs[:LOADS], 0.0)
        turned = jnp.where(lane16 < LOADS, pltpu.roll(gs[LOADS:], 112, 1), 0.0)
        sym = plain + turned
        plain = plain + plain
        ra[n, chip_pos] = (
            plain[:8] + pltpu.roll(plain[8:], 16, 1) + pltpu.roll(sym[:8], 32, 1) + pltpu.roll(sym[8:], 48, 1)
        )
        for k in range(1, 2 * NROW):
            pos = lax.rem(chip_pos + k, 2 * NROW)
            pltpu.make_async_remote_copy(
                src_ref=ra.at[n, chip_pos],
                dst_ref=ra.at[n, chip_pos],
                send_sem=send.at[ARA + n],
                recv_sem=recv.at[ARA + n],
                device_id=(2 * chip_id + pos // NROW, lax.rem(pos, NROW)),
                device_id_type=MESH,
            ).start()

    def tree(values):
        while len(values) > 1:
            values = [a + b for a, b in zip(values[::2], values[1::2])]
        return values[0]

    def inner_middle(n):
        arrived(ra.at[n, pl.ds(0, 2 * NROW - 1)], ARA + n)
        rb[n, chip_id] = tree([ra[n, i] for i in range(2 * NROW)])

        @pl.loop(1, NSUB // 2)
        def _(k):
            far = lax.rem(chip_id + k, NSUB // 2)
            pltpu.make_async_remote_copy(
                src_ref=rb.at[n, chip_id],
                dst_ref=rb.at[n, chip_id],
                send_sem=send.at[ARB + n],
                recv_sem=recv.at[ARB + n],
                device_id=(2 * far + core, q),
                device_id_type=MESH,
            ).start()

    def inner_finish(n):
        arrived(rb.at[n, pl.ds(0, NSUB // 2 - 1)], ARB + n)
        total = tree([rb[n, i] for i in range(NSUB // 2)])
        plain = jnp.concatenate([total, pltpu.roll(total, 112, 1)], axis=0)
        sym = jnp.concatenate([pltpu.roll(total, 96, 1), pltpu.roll(total, 80, 1)], axis=0)
        return plain, sym

    def solve(a, b):
        return eliminate(
            jnp.where(lane16 < LOADS, a, jnp.where(lane16 < 2 * LOADS, pltpu.roll(b, 16, 1), 0.0))
        )

    def combine(x, coeffs):
        small = coeffs[:, :LOADS]
        return jnp.concatenate(
            [dot_tn(small, x[:LOADS], HIGHEST), dot_tn(small, x[LOADS:], HIGHEST)], axis=0
        )

    v = corner_finish(0, rv[...])
    jump_send(0, v)
    rv[...] = jump_finish(0, v)

    gather_x(0, rv[...])
    for f in range(FACES):
        pltpu.make_async_copy(
            s_hbm.at[:, pl.ds(FACEQ * f, FACEQ), :], sv.at[:, pl.ds(128 * f, FACEQ), :], s_sem.at[f]
        ).wait()
    y = product(0, sv)
    jump_send(1, y)
    inner_start(0, rv[...], y)
    dv[...] = jump_finish(1, y)

    gather_x(1, dv[...])
    corner_send(1, dot_nt(xb[1], hcf[:, :KMAIN]))
    inner_middle(0)
    flex = product(1, hv)
    v = corner_finish(1, flex)
    inner_start(1, dv[...], v)
    jump_send(2, v)
    energy, energy_sym = inner_finish(0)
    inner_middle(1)
    image = jump_finish(2, v)
    unused, curvature = inner_finish(1)
    step = solve(curvature, energy)
    rv[...] = rv[...] - combine(image, step)
    gather_x(2, rv[...])
    y = product(2, sv)
    inner_start(2, rv[...], y)
    jump_send(3, y)
    mv[...] = combine(dv[...], step)
    inner_middle(2)
    zvec = jump_finish(3, y)
    energy_next, unused = inner_finish(2)
    blend = solve(energy_sym, energy_next)
    dv[...] = zvec + combine(dv[...], blend)

    gather_x(3, dv[...])
    corner_send(2, dot_nt(xb[3], hcf[:, :KMAIN]))
    flex = product(3, hv)
    v = corner_finish(2, flex)
    inner_start(3, dv[...], v)
    jump_send(4, v)
    inner_middle(3)
    image = jump_finish(4, v)
    unused, curvature = inner_finish(3)
    step = solve(curvature, energy_next)

    def put_out(ref, value):
        tiles = pack_tiles([value[:, 128 * f : 128 * f + 128] for f in range(FACES)], 0, 5)
        for s in range(2):
            for t in range(5):
                ref[s, :, 128 * t : 128 * t + 128] = tiles[t][LOADS * s : LOADS * s + LOADS]
            ref[s, :, PART:BLOCK] = jnp.zeros((LOADS, BLOCK - PART), F32)

    put_out(mult_out, mv[...] + combine(dv[...], step))
    put_out(res_out, rv[...] - combine(image, step))

    for ref, sem in drains:
        pltpu.make_async_copy(ref, ref, send.at[sem]).wait()


def body(
    forces, inverse_h, schur_matrix, coarse_inv, face_perm, corner_rows, corner_ids, corner_count
):
    fpad = jnp.pad(forces, ((0, 0), (0, 0), (0, SPILL - BLOCK))).reshape(2 * LOADS, SPILL)
    h_tail = jnp.pad(inverse_h[:, FACES * FACEQ :, :], ((0, 0), (0, 128 - (BLOCK - FACES * FACEQ)), (0, 0)))
    perm = jnp.pad(face_perm, ((0, 0), (0, 0), (0, 128 - FACEQ)), constant_values=127).reshape(12, 128)
    none = jnp.full((24,), -1, jnp.int32)
    cr = jnp.stack(
        [jnp.concatenate([corner_rows[0], none]), jnp.concatenate([none, corner_rows[1]])]
    )[..., None]
    live = jnp.where(jnp.arange(24)[None, :] < corner_count[:, None], corner_ids, -1).reshape(SLOTS)
    ids = jnp.concatenate([live, live, jnp.full((32,), -1, jnp.int32)])
    ids = jnp.broadcast_to(ids[None, :], (8, 128))

    vmem = pl.BlockSpec(memory_space=pltpu.VMEM)
    hbm = pl.BlockSpec(memory_space=pl.ANY)
    out = jax.ShapeDtypeStruct((2, LOADS, BLOCK), F32)
    return pl.pallas_call(
        kernel,
        out_shape=(out, out),
        in_specs=[vmem, hbm, hbm, vmem, vmem, vmem, vmem, vmem],
        out_specs=(vmem, vmem),
        scratch_shapes=[
            pltpu.VMEM((2, WIDE, NS), BF16),
            pltpu.VMEM((2, WIDE, NS), BF16),
            pltpu.VMEM((NSUB, 8, 128), jnp.int32),
            pltpu.VMEM((NSUB, 8, 128), F32),
            pltpu.VMEM((NROW, NSUB, 8, 128), F32),
            pltpu.VMEM((SLOTS, 1024), F32),
            pltpu.VMEM((128, NSUB * 128), BF16),
            pltpu.VMEM((NROW, 32, SPILL), BF16),
            pltpu.VMEM((32, KFULL), BF16),
            pltpu.VMEM((2, LOADS + SLOTS, KFULL), BF16),
            pltpu.VMEM((128, WIDE), BF16),
            pltpu.VMEM((NROW, SLOTS, SPILL), BF16),
            pltpu.VMEM((128, KFULL), BF16),
            pltpu.VMEM((4, 32, KMAIN), BF16),
            pltpu.VMEM((3, LOADS, NSUB * 128), BF16),
            pltpu.VMEM((5, 10, LOADS, 128), F32),
            pltpu.VMEM((5, 10, LOADS, 128), F32),
            pltpu.VMEM((4, 2 * NROW, 8, 128), F32),
            pltpu.VMEM((4, NSUB // 2, 8, 128), F32),
            pltpu.VMEM((32, 128), F32),
            pltpu.VMEM((12, LOADS, 128), jnp.int32),
            pltpu.VMEM((32, WIDE), F32),
            pltpu.VMEM((32, WIDE), F32),
            pltpu.VMEM((32, WIDE), F32),
            pltpu.SemaphoreType.DMA((FACES,)),
            pltpu.SemaphoreType.DMA((FACES,)),
            pltpu.SemaphoreType.DMA((NSEM,)),
            pltpu.SemaphoreType.DMA((NSEM,)),
        ],
        compiler_params=pltpu.CompilerParams(
            collective_id=0, has_side_effects=True, vmem_limit_bytes=48 * 1024 * 1024
        ),
    )(fpad, inverse_h, schur_matrix, h_tail, coarse_inv, perm, cr, ids)


def solution(mesh):
    in_specs = (
        P("sub", None, "row"),
        P("sub", "row", None),
        P("sub", "row", None),
        P(("sub", "row"), None),
        P("sub", None, "row"),
        P("sub", None),
        P("sub", None),
        P("sub"),
    )
    out_specs = (P("sub", None, "row"), P("sub", None, "row"))
    return jax.shard_map(body, mesh=mesh, in_specs=in_specs, out_specs=out_specs, check_vma=False)
```

time: 1420 us -> 130 us (0.09)
  waiting for transfers between devices: 1050 us -> 0 us
  blocking collectives: 198 us -> 0 us
  Pallas kernels: 0 us -> 111 us
  starting transfers between devices: 82.1 us -> 0 us
  matrix products: 52.7 us -> 0 us
  between operations: 15.4 us -> 0.68 us
  other arithmetic: 15.2 us -> 0.84 us
    unnamed x19 -> x0, waiting for transfers between devices: 625 us -> none
    psum x3 -> x0, waiting for transfers between devices: 412 us -> none  [coarse_term(): coarse = lax.psum(partial_coarse, ('sub', 'row'))]
    psum x3 -> x0, blocking collectives: 198 us -> none  [inner_products(): lax.psum(jnp.einsum('sik,sjk->ij', left, right, precision=HIGHEST), ('sub...]
    pallas_call x0 -> x1, Pallas kernels: none -> 111 us  [body(): pl.pallas_call(kernel, out_shape=(out, out), in_specs=[vmem, hbm, hbm, vm...]
    ppermute x40 -> x0, starting transfers between devices: 81.6 us -> none  [the longest x20 56.1 us: from_behind(): lax.ppermute(value, axis, [(source, source + steps) for source in range(l...]
    dot_general x35 -> x0, matrix products: 51.5 us -> none  [the longest x5 24 us: block_product(): jnp.einsum('srb,sbk->srk', rounded, matrices, preferred_element_type=jnp....]
    unnamed x19 -> x9, local copies, waits for them, and re-layouts: 0.64 us -> 14.9 us
  transfers between devices with their start and end apart: 51 -> 0, of which waited for: 26 -> 0; matrix products, arithmetic and copies ran while one was open for 1% -> 0% of each run, Pallas kernels for 0% -> 0%
where the time goes in v1:
time: 130 us
  Pallas kernels  111 us (85%)
  local copies, waits for them, and re-layouts  17 us (13%)
    pallas_call x1, Pallas kernels, body(): pl.pallas_call(kernel, out_shape=(out, out), in_specs=[vmem, hbm, hbm, vm...  111 us
    unnamed x9, local copies, waits for them, and re-layouts  14.9 us

profile of v1, /device:TPU:1, one launch (start us, length us, event | category | flops | bytes accessed | tf_op | source)
XLA Modules:
  0.0 129.5 jit_solution(15667168286535706688)
XLA Ops:
  0.6 0.8 compare_select_fusion
  1.4 0.1 reshape.17
  1.5 0.1 pad_add_fusion
  1.5 0.8 slice_bitcast_fusion.1
  2.3 0.1 pad_bitcast_fusion
  2.4 0.7 copy.20
  3.1 0.1 copy.19.cr
  3.2 0.9 pad.14
  4.1 3.8 %copy.17.h_hbm = bf16[2,650,2600]{2,1,0:T(8,128)(2,1)S(1)} copy(bf16[2,650,2600]{2,0,1:T(2,128)(2,1)} %param.9) | data formatting | bytes 13520000 | tf_op args[1]
  7.9 0.0 copy-start.1
  7.9 0.1 slice.12
  8.0 0.1 pad.15.h_tail
  8.1 0.0 copy-start
  8.1 9.1 %copy.18.s_hbm = bf16[2,650,2600]{2,1,0:T(8,128)(2,1)} copy(bf16[2,650,2600]{2,0,1:T(2,128)(2,1)} %param.10) | data formatting | bytes 13520000 | tf_op args[2]
  17.3 0.0 copy-done.1
  17.3 0.0 copy-done
  17.3 110.9 %shard_map.95 = (f32[2,16,650]{2,1,0:T(8,128)S(1)}, f32[2,16,650]{2,1,0:T(8,128)S(1)}) custom-call(f32[32,768]{1,0:T(8,128)S(1)} %bitcast.11, bf16[2,650,2600]{2,1,0:T(8,128)(2,1)} %copy-done.1, bf16[2,650,2600]{2,1,0:T(8,128)(2,1)} %copy.18.s_hbm, bf16[2,128,2600]{2,1,0:T(8,128)(2,1)S(1)} %pad.15.h_tail, f32[8,1024]{1,0:T(8,128)S(1)} %copy-done, ...), custom_call_target="tpu_custom_call" | custom-call | tf_op jit(solution)/shard_map/pallas_call | solution.py:534
  128.2 0.6 copy.23
  128.9 0.6 copy.24
  (5 shorter events, 0.0 us)
Async XLA Ops:
  7.9 9.3 %copy-start.1 = (bf16[2,650,2600]{2,1,0:T(8,128)(2,1)}, bf16[2,650,2600]{2,1,0:T(8,128)(2,1)S(1)}, u32[]{:S(2)}) copy-start(bf16[2,650,2600]{2,1,0:T(8,128)(2,1)S(1)} %copy.17.h_hbm) | copy-start | bytes 20280004
  8.1 9.2 %copy-start = (f32[8,1024]{1,0:T(8,128)S(1)}, f32[8,1024]{1,0:T(8,128)}, u32[]{:S(2)}) copy-start(f32[8,1024]{1,0:T(8,128)} %c_own.1) | copy-start | bytes 98308

commit v2 on v1

--- a/solution.py
+++ b/solution.py
@@ -27,7 +27,8 @@
 SLOTS = 48
 
 IDS, FORCES, TPART, CFULL, HCORN, XG, CORN, JUMP, ARA, ARB = 0, 1, 2, 3, 4, 5, 9, 12, 17, 21
-NSEM = 25
+XL = 25
+NSEM = 29
 
 
 def lanes(shape):
@@ -86,20 +87,27 @@
 
 
 def eliminate(m):
-    row_id = lax.broadcasted_iota(jnp.int32, (LOADS, 128), 0)
+    wide = (LOADS, 128)
+    row_id = lax.broadcasted_iota(jnp.int32, wide, 0)
+    cols = [jnp.broadcast_to(m[:, k : k + 1], wide) for k in range(LOADS)]
     for k in range(LOADS):
-        col = jnp.broadcast_to(m[:, k : k + 1], (LOADS, 128))
-        row = jnp.broadcast_to(m[k : k + 1, :], (LOADS, 128))
-        pivot = jnp.broadcast_to(col[k : k + 1, :], (LOADS, 128))
-        row = row / pivot
-        m = jnp.where(row_id == k, row, m - col * row)
+        scale = 1.0 / jnp.broadcast_to(cols[k][k : k + 1, :], wide)
+
+        def step(x):
+            row = jnp.broadcast_to(x[k : k + 1, :], wide) * scale
+            return jnp.where(row_id == k, row, x - cols[k] * row)
+
+        m = step(m)
+        for j in range(k + 1, LOADS):
+            cols[j] = step(cols[j])
     return pltpu.roll(m, 112, 1)
 
 
 def kernel(
-    forces, h_hbm, s_hbm, h_tail, c_own, perm, cr, ids, mult_out, res_out,
-    hv, sv, ib, tb, ca, cat, kt, fb, xf, lhs, hco, hcb, hcf, xb, cb, sb, jb, ra, rb, gs, pidx, dv, rv, mv,
-    h_sem, s_sem, send, recv,
+    forces_in, h_hbm, s_hbm, c_in, perm_in, rows_in, ids_in, count_in, mult_out, res_out,
+    forces, c_own, perm, corner_rows, corner_ids, count,
+    raw_h, raw_s, hv, sv, ht, ib, tb, ca, cat, kt, fb, ft, xf, oh, hco, hcb, hcf, xb, xl, xw, cb, sb, jb, ra, rb, gs, pidx,
+    small, dv, rv, mv, in_sem, h_sem, s_sem, send, recv,
 ):
     g = lax.axis_index("sub")
     q = lax.axis_index("row")
@@ -110,14 +118,22 @@
     def dev(x, z, c):
         return (x * 4 + z) * 2 + c
 
-    for f in range(FACES):
-        pltpu.make_async_copy(
-            h_hbm.at[:, pl.ds(FACEQ * f, FACEQ), :], hv.at[:, pl.ds(128 * f, FACEQ), :], h_sem.at[f]
-        ).start()
-    for f in range(FACES):
-        pltpu.make_async_copy(
-            s_hbm.at[:, pl.ds(FACEQ * f, FACEQ), :], sv.at[:, pl.ds(128 * f, FACEQ), :], s_sem.at[f]
-        ).start()
+    def load(src, dst, sem, f):
+        size = FACEQ if f < FACES else BLOCK - FACES * FACEQ
+        rows = pl.ds(FACEQ * f, size)
+        return pltpu.make_async_copy(src.at[rows], dst.at[rows], sem.at[f])
+
+    inputs = [
+        pltpu.make_async_copy(src, dst, in_sem.at[i])
+        for i, (src, dst) in enumerate(
+            [(ids_in, corner_ids), (count_in, count), (forces_in, forces), (rows_in, corner_rows)]
+            + [(c_in, c_own), (perm_in, perm)]
+        )
+    ]
+    for copy in inputs:
+        copy.start()
+    for f in range(FACES + 1):
+        load(h_hbm, raw_h, h_sem, f).start()
 
     barrier = pltpu.get_barrier_semaphore()
 
@@ -133,28 +149,65 @@
         pl.semaphore_signal(barrier, inc=1, device_id=(g, far), device_id_type=MESH)
         pl.semaphore_signal(barrier, inc=1, device_id=(other, far), device_id_type=MESH)
 
-    for half in (hv, sv):
-        for s in range(2):
-            for f in range(FACES):
-                half[s, 128 * f + FACEQ : 128 * f + 128, :] = jnp.zeros((32, NS), BF16)
-    for i in range(12):
-        pidx[i] = jnp.broadcast_to(perm[i : i + 1, :], (LOADS, 128))
-    hco[...] = jnp.zeros((128, WIDE), BF16)
-    hcf[96:128, :] = jnp.zeros((32, KFULL), BF16)
-    kt[96:128, :] = jnp.zeros((32, NSUB * 128), BF16)
-    gs[...] = jnp.zeros((32, 128), F32)
-    for s in range(2):
-        spot = jnp.broadcast_to(cr[s], (SLOTS, KFULL))
-        lhs[s, LOADS:, :] = jnp.where(lanes((SLOTS, KFULL)) == spot, 1.0, 0.0).astype(BF16)
-
-    ib[g] = ids[...]
+    for f in range(FACES):
+        load(s_hbm, raw_s, s_sem, f).start()
+
+    for copy in inputs:
+        copy.wait()
+    lane8 = lanes((8, 128))
+
+    def slot_row(ref, first, second):
+        small[...] = jnp.full((8, 128), -1, jnp.int32)
+        small[0:2, 0:24] = ref[...]
+        top = jnp.broadcast_to(small[0:1, :], (8, 128))
+        low = pltpu.roll(jnp.broadcast_to(small[1:2, :], (8, 128)), 24, 1)
+        out = jnp.where(lane8 < first, top, -1)
+        return jnp.where((lane8 >= 24) & (lane8 < 24 + second), low, out)
+
+    live = slot_row(corner_ids, jnp.minimum(count[0], 24), jnp.minimum(count[1], 24))
+    both = pltpu.roll(live, SLOTS, 1)
+    ib[g] = jnp.where(lane8 < SLOTS, live, jnp.where(lane8 < 2 * SLOTS, both, -1))
+
     shift = 10 * q
     lane32 = lanes((32, 128))
     last = jnp.zeros((32, 128), F32)
+    ft[...] = last
+    for s in range(2):
+        ft[LOADS * s : LOADS * s + LOADS, 0 : BLOCK - PART] = forces[s, :, PART:BLOCK]
     for t in range(6):
-        now = pltpu.roll(forces[:, 128 * t : 128 * t + 128], shift, 1)
+        if t < 5:
+            now = jnp.concatenate([forces[s, :, 128 * t : 128 * t + 128] for s in range(2)], axis=0)
+        else:
+            now = ft[...]
+        now = pltpu.roll(now, shift, 1)
         fb[q, :, 128 * t : 128 * t + 128] = jnp.where(lane32 >= shift, now, last).astype(BF16)
         last = now
+
+    rows = slot_row(corner_rows, 24, 24).astype(F32)
+    spot = jnp.broadcast_to(rows[0:1, :], (128, 128)).T[:SLOTS].astype(jnp.int32)
+    lane48 = lanes((SLOTS, 128))
+    upper = lax.broadcasted_iota(jnp.int32, (SLOTS, 128), 0) < 24
+    for t in range(KFULL // 128):
+        hit = jnp.where(lane48 + 128 * t == spot, 1.0, 0.0)
+        oh[0, :, 128 * t : 128 * t + 128] = jnp.where(upper, hit, 0.0).astype(BF16)
+        oh[1, :, 128 * t : 128 * t + 128] = jnp.where(upper, 0.0, hit).astype(BF16)
+    for s in range(2):
+        for f in range(FACES):
+            hv[s, 128 * f + FACEQ : 128 * f + 128, :] = jnp.zeros((32, NS), BF16)
+    hco[...] = jnp.zeros((128, WIDE), BF16)
+
+    def split(raw, start, dst, at, count):
+        @pl.loop(0, count)
+        def _(i):
+            pair = jnp.swapaxes(raw[pl.ds(start + 16 * i, 16)], 0, 1)
+            for s in range(2):
+                dst[s, pl.ds(pl.multiple_of(at + 16 * i, 16), 16), :] = pair[s]
+
+    for f in range(FACES):
+        load(h_hbm, raw_h, h_sem, f).wait()
+        split(raw_h, FACEQ * f, hv, 128 * f, FACEQ // 16)
+    load(h_hbm, raw_h, h_sem, FACES).wait()
+    split(raw_h, FACEQ * FACES, ht, 0, 5)
 
     pl.semaphore_wait(barrier, NSUB - 1 + 2 * (NROW - 1))
 
@@ -191,6 +244,20 @@
     to_plane(lambda far: ib.at[g], ib.at[g], IDS)
     to_row(fb.at[q], FORCES)
 
+    corner_h = jnp.zeros((SLOTS, WIDE), F32)
+    corner_t = jnp.zeros((SLOTS, 128), F32)
+    for s in range(2):
+        corner_h = corner_h + dot_nt(oh[s, :, :KMAIN], hv[s, :, :KMAIN])
+        corner_h = corner_h + dot_nt(oh[s, :, KMAIN:NS], hv[s, :, KMAIN:NS])
+        corner_t = corner_t + dot_nt(oh[s, :, :KMAIN], ht[s, :, :KMAIN])
+        corner_t = corner_t + dot_nt(oh[s, :, KMAIN:NS], ht[s, :, KMAIN:NS])
+    corner_t = jnp.where(lane48 < BLOCK - FACES * FACEQ, corner_t, 0.0)
+    hco[:SLOTS, :] = corner_h.astype(BF16)
+    pieces = [corner_h[:, 128 * f : 128 * f + 128] for f in range(FACES)] + [corner_t]
+    for t, tile in enumerate(pack_tiles(pieces, shift, 6)):
+        hcb[q, :, 128 * t : 128 * t + 128] = tile.astype(BF16)
+    to_row(hcb.at[q], HCORN)
+
     arrived(ib.at[pl.ds(0, NSUB - 1)], IDS)
 
     def pick_columns(far):
@@ -203,7 +270,7 @@
             total = total + jnp.where(tile == v, got, 0.0)
         return total
 
-    ca[q, g] = pick_columns(g)
+    ca[g] = pick_columns(g)
 
     @pl.loop(1, NSUB)
     def _(k):
@@ -211,7 +278,7 @@
         tb[far] = pick_columns(far)
         pltpu.make_async_remote_copy(
             src_ref=tb.at[far],
-            dst_ref=ca.at[q, g],
+            dst_ref=ca.at[g],
             send_sem=send.at[TPART],
             recv_sem=recv.at[TPART],
             device_id=(far, q),
@@ -230,43 +297,12 @@
     arrived(fb.at[pl.ds(0, NROW - 1)], FORCES)
 
     def put_forces(start, value):
-        width = value.shape[1]
-        xf[:, start : start + width] = value
-        lhs[0, :LOADS, start : start + width] = value[:LOADS]
-        lhs[1, :LOADS, start : start + width] = value[LOADS:]
+        xf[:, start : start + value.shape[1]] = value
 
     assemble(fb, put_forces)
 
-    for f in range(FACES):
-        pltpu.make_async_copy(
-            h_hbm.at[:, pl.ds(FACEQ * f, FACEQ), :], hv.at[:, pl.ds(128 * f, FACEQ), :], h_sem.at[f]
-        ).wait()
-
-    flex0 = []
-    corner_h = jnp.zeros((SLOTS, WIDE), F32)
-    corner_t = jnp.zeros((SLOTS, 128), F32)
-    for s in range(2):
-        prod = dot_nt(lhs[s, :, :KMAIN], hv[s, :, :KMAIN]) + dot_nt(
-            lhs[s, :, KMAIN:NS], hv[s, :, KMAIN:NS]
-        )
-        tail = dot_nt(lhs[s, LOADS:, :KMAIN], h_tail[s, :, :KMAIN]) + dot_nt(
-            lhs[s, LOADS:, KMAIN:NS], h_tail[s, :, KMAIN:NS]
-        )
-        flex0.append(prod[:LOADS])
-        corner_h = corner_h + prod[LOADS:]
-        corner_t = corner_t + tail
-    flex0 = jnp.concatenate(flex0, axis=0)
-    rv[...] = flex0
-    hco[:SLOTS, :] = corner_h.astype(BF16)
-    pieces = [corner_h[:, 128 * f : 128 * f + 128] for f in range(FACES)] + [corner_t]
-    for t, tile in enumerate(pack_tiles(pieces, shift, 6)):
-        hcb[q, :, 128 * t : 128 * t + 128] = tile.astype(BF16)
-    to_row(hcb.at[q], HCORN)
-
-    arrived(ca.at[0, pl.ds(0, NSUB - 1)], TPART)
-    to_row(ca.at[q], CFULL)
-
     arrived(hcb.at[pl.ds(0, NROW - 1)], HCORN)
+    hcf[96:128, :] = jnp.zeros((32, KFULL), BF16)
 
     def put_corner(start, value):
         width = value.shape[1]
@@ -287,31 +323,56 @@
 
     corner_send(0, dot_nt(xf[...], hcf[...]))
 
-    arrived(ca.at[pl.ds(0, NROW - 1)], CFULL)
-    for p in range(NROW):
-        for half in range(2):
-            block = ca[p, 16 * half : 16 * half + 16].reshape(128, 128)
-            spot = (2 * p + half) * 128
-            cat[:, spot : spot + 128] = block.T[:SLOTS]
-
-    @pl.loop(0, NSUB)
-    def _(far):
-        c = ib[far]
+    arrived(ca.at[pl.ds(0, NSUB - 1)], TPART)
+    for half in range(2):
+        block = ca[16 * half : 16 * half + 16].reshape(128, 128)
+        cat[q, :, 128 * half : 128 * half + 128] = block.T[:SLOTS]
+    to_row(cat.at[q], CFULL)
+
+    for s in range(2):
+        rv[LOADS * s : LOADS * s + LOADS, :] = dot_nt(
+            xf[LOADS * s : LOADS * s + LOADS, :KMAIN], hv[s, :, :KMAIN]
+        ) + dot_nt(xf[LOADS * s : LOADS * s + LOADS, KMAIN:NS], hv[s, :, KMAIN:NS])
+
+    for f in range(FACES):
+        for t in range(2):
+            pidx[FACES * t + f] = jnp.full((LOADS, 128), 127, jnp.int32)
+            pidx[FACES * t + f, :, :FACEQ] = jnp.broadcast_to(perm[f, t : t + 1, :], (LOADS, FACEQ))
+    kt[96:128, :] = jnp.zeros((32, NSUB * 128), BF16)
+    gs[...] = jnp.zeros((32, 128), F32)
+    for s in range(2):
+        for f in range(FACES):
+            sv[s, 128 * f + FACEQ : 128 * f + 128, :] = jnp.zeros((32, NS), BF16)
+    for f in range(FACES):
+        load(s_hbm, raw_s, s_sem, f).wait()
+        split(raw_s, FACEQ * f, sv, 128 * f, FACEQ // 16)
+
+    arrived(cat.at[pl.ds(0, NROW - 1)], CFULL)
+
+    slot_lane = lanes((SLOTS, 128))
+
+    @pl.loop(0, NSUB // 2)
+    def _(pair):
+        c = jnp.where(lane8 < SLOTS, ib[2 * pair], ib[2 * pair + 1])
         tile = 2 * lax.bitwise_and(lax.shift_right_arithmetic(c, 3), 3) + lax.shift_right_arithmetic(c, 9)
         tile = jnp.where(c < 0, -1, tile)
         lane = 8 * lax.bitwise_and(lax.shift_right_arithmetic(c, 5), 15) + lax.bitwise_and(c, 7)
-        cols = pl.ds(pl.multiple_of(128 * far, 128), 128)
         parts = []
         for a in range(SLOTS // 8):
             total = jnp.zeros((8, 128), F32)
             for v in range(8):
-                got = lane_gather(cat[8 * a : 8 * a + 8, 128 * v : 128 * v + 128], lane)
+                got = lane_gather(cat[v // 2, 8 * a : 8 * a + 8, 128 * (v % 2) : 128 * (v % 2) + 128], lane)
                 total = total + jnp.where(tile == v, got, 0.0)
             parts.append(total)
         total = jnp.concatenate(parts, axis=0)
-        high = total.astype(BF16)
-        kt[:SLOTS, cols] = high
-        kt[SLOTS : 2 * SLOTS, cols] = (total - high.astype(F32)).astype(BF16)
+        first = jnp.where(slot_lane < SLOTS, total, pltpu.roll(total, SLOTS, 1))
+        second = jnp.where(slot_lane < SLOTS, pltpu.roll(total, 128 - SLOTS, 1), total)
+        for i, part in enumerate((first, second)):
+            part = jnp.where(slot_lane < 2 * SLOTS, part, 0.0)
+            high = part.astype(BF16)
+            cols = pl.ds(pl.multiple_of(256 * pair + 128 * i, 128), 128)
+            kt[:SLOTS, cols] = high
+            kt[SLOTS : 2 * SLOTS, cols] = (part - high.astype(F32)).astype(BF16)
 
     def corner_finish(n, flex):
         arrived(cb.at[n, :, pl.ds(0, (NSUB - 1) * 128)], CORN + n)
@@ -370,16 +431,27 @@
 
     own_part = pl.ds(pl.multiple_of(PART * q, 128), PART)
 
-    def gather_x(n, x):
+    def gather_send(n, x):
         pieces = [x[:, 128 * f : 128 * f + 128] for f in range(FACES)]
-        tiles = pack_tiles(pieces, shift, 5)
-        xb[n, :, own_part] = jnp.concatenate(tiles, axis=1).astype(BF16)
+        whole = jnp.concatenate(pack_tiles(pieces, shift, 5), axis=1)
+        high = whole.astype(BF16)
+        xb[n, :, own_part] = high
         to_row(xb.at[n, :, own_part], XG + n)
+        xl[n, :, own_part] = (whole - high.astype(F32)).astype(BF16)
+        to_row(xl.at[n, :, own_part], XL + n)
+
+    def gather_high(n):
         arrived(xb.at[n, :, pl.ds(0, 3 * PART)], XG + n)
 
-    def product(n, mat):
+    def gather_low(n):
+        arrived(xl.at[n, :, pl.ds(0, 3 * PART)], XL + n)
+
+    def full(n):
+        return xb[n].astype(F32) + xl[n].astype(F32)
+
+    def product(x, mat):
         return jnp.concatenate(
-            [dot_nt(xb[n, :LOADS, :], mat[0, :, :KMAIN]), dot_nt(xb[n, LOADS:, :], mat[1, :, :KMAIN])],
+            [dot_nt(x[:LOADS, :], mat[0, :, :KMAIN]), dot_nt(x[LOADS:, :], mat[1, :, :KMAIN])],
             axis=0,
         )
 
@@ -455,43 +527,51 @@
     jump_send(0, v)
     rv[...] = jump_finish(0, v)
 
-    gather_x(0, rv[...])
-    for f in range(FACES):
-        pltpu.make_async_copy(
-            s_hbm.at[:, pl.ds(FACEQ * f, FACEQ), :], sv.at[:, pl.ds(128 * f, FACEQ), :], s_sem.at[f]
-        ).wait()
-    y = product(0, sv)
+    gather_send(0, rv[...])
+    gather_high(0)
+    y = product(xb.at[0], sv)
     jump_send(1, y)
     inner_start(0, rv[...], y)
     dv[...] = jump_finish(1, y)
 
-    gather_x(1, dv[...])
+    gather_send(1, dv[...])
+    gather_low(0)
+    gather_high(1)
     corner_send(1, dot_nt(xb[1], hcf[:, :KMAIN]))
     inner_middle(0)
-    flex = product(1, hv)
+    flex = product(xb.at[1], hv)
     v = corner_finish(1, flex)
+    jump_send(2, v)
     inner_start(1, dv[...], v)
-    jump_send(2, v)
+    gather_low(1)
     energy, energy_sym = inner_finish(0)
+    row16 = lax.broadcasted_iota(jnp.int32, (LOADS, 128), 0)
+    energy_inv = solve(energy_sym, jnp.where(row16 == lane16, 1.0, 0.0))
+    image = jump_finish(2, v)
+    gather_send(2, image)
     inner_middle(1)
-    image = jump_finish(2, v)
     unused, curvature = inner_finish(1)
     step = solve(curvature, energy)
     rv[...] = rv[...] - combine(image, step)
-    gather_x(2, rv[...])
-    y = product(2, sv)
+    gather_high(2)
+    gather_low(2)
+    xw[0] = (full(0) - combine(full(2), step)).astype(BF16)
+    y = product(xw.at[0], sv)
+    jump_send(3, y)
     inner_start(2, rv[...], y)
-    jump_send(3, y)
     mv[...] = combine(dv[...], step)
+    zvec = jump_finish(3, y)
+    gather_send(3, zvec)
     inner_middle(2)
-    zvec = jump_finish(3, y)
     energy_next, unused = inner_finish(2)
-    blend = solve(energy_sym, energy_next)
+    blend = dot_nn(energy_inv[:, :LOADS], energy_next[:, :LOADS], HIGHEST)
     dv[...] = zvec + combine(dv[...], blend)
 
-    gather_x(3, dv[...])
-    corner_send(2, dot_nt(xb[3], hcf[:, :KMAIN]))
-    flex = product(3, hv)
+    gather_high(3)
+    gather_low(3)
+    xw[1] = (full(3) + combine(full(1), blend)).astype(BF16)
+    corner_send(2, dot_nt(xw[1], hcf[:, :KMAIN]))
+    flex = product(xw.at[1], hv)
     v = corner_finish(2, flex)
     inner_start(3, dv[...], v)
     jump_send(4, v)
@@ -517,40 +597,44 @@
 def body(
     forces, inverse_h, schur_matrix, coarse_inv, face_perm, corner_rows, corner_ids, corner_count
 ):
-    fpad = jnp.pad(forces, ((0, 0), (0, 0), (0, SPILL - BLOCK))).reshape(2 * LOADS, SPILL)
-    h_tail = jnp.pad(inverse_h[:, FACES * FACEQ :, :], ((0, 0), (0, 128 - (BLOCK - FACES * FACEQ)), (0, 0)))
-    perm = jnp.pad(face_perm, ((0, 0), (0, 0), (0, 128 - FACEQ)), constant_values=127).reshape(12, 128)
-    none = jnp.full((24,), -1, jnp.int32)
-    cr = jnp.stack(
-        [jnp.concatenate([corner_rows[0], none]), jnp.concatenate([none, corner_rows[1]])]
-    )[..., None]
-    live = jnp.where(jnp.arange(24)[None, :] < corner_count[:, None], corner_ids, -1).reshape(SLOTS)
-    ids = jnp.concatenate([live, live, jnp.full((32,), -1, jnp.int32)])
-    ids = jnp.broadcast_to(ids[None, :], (8, 128))
-
+    h = jnp.transpose(inverse_h, (1, 0, 2))
+    schur = jnp.transpose(schur_matrix, (1, 0, 2))
+    perm = jnp.transpose(face_perm, (1, 0, 2))
     vmem = pl.BlockSpec(memory_space=pltpu.VMEM)
-    hbm = pl.BlockSpec(memory_space=pl.ANY)
+    hbm = pl.BlockSpec(memory_space=pltpu.MemorySpace.HBM)
     out = jax.ShapeDtypeStruct((2, LOADS, BLOCK), F32)
     return pl.pallas_call(
         kernel,
         out_shape=(out, out),
-        in_specs=[vmem, hbm, hbm, vmem, vmem, vmem, vmem, vmem],
+        in_specs=[hbm] * 8,
         out_specs=(vmem, vmem),
         scratch_shapes=[
+            pltpu.VMEM((2, LOADS, BLOCK), F32),
+            pltpu.VMEM((8, 1024), F32),
+            pltpu.VMEM((FACES, 2, FACEQ), jnp.int32),
+            pltpu.VMEM((2, 24), jnp.int32),
+            pltpu.VMEM((2, 24), jnp.int32),
+            pltpu.SMEM((2,), jnp.int32),
+            pltpu.VMEM((656, 2, NS), BF16),
+            pltpu.VMEM((FACES * FACEQ, 2, NS), BF16),
             pltpu.VMEM((2, WIDE, NS), BF16),
             pltpu.VMEM((2, WIDE, NS), BF16),
+            pltpu.VMEM((2, 128, NS), BF16),
             pltpu.VMEM((NSUB, 8, 128), jnp.int32),
             pltpu.VMEM((NSUB, 8, 128), F32),
-            pltpu.VMEM((NROW, NSUB, 8, 128), F32),
-            pltpu.VMEM((SLOTS, 1024), F32),
+            pltpu.VMEM((NSUB, 8, 128), F32),
+            pltpu.VMEM((NROW, SLOTS, 256), F32),
             pltpu.VMEM((128, NSUB * 128), BF16),
             pltpu.VMEM((NROW, 32, SPILL), BF16),
+            pltpu.VMEM((32, 128), F32),
             pltpu.VMEM((32, KFULL), BF16),
-            pltpu.VMEM((2, LOADS + SLOTS, KFULL), BF16),
+            pltpu.VMEM((2, SLOTS, KFULL), BF16),
             pltpu.VMEM((128, WIDE), BF16),
             pltpu.VMEM((NROW, SLOTS, SPILL), BF16),
             pltpu.VMEM((128, KFULL), BF16),
             pltpu.VMEM((4, 32, KMAIN), BF16),
+            pltpu.VMEM((4, 32, KMAIN), BF16),
+            pltpu.VMEM((2, 32, KMAIN), BF16),
             pltpu.VMEM((3, LOADS, NSUB * 128), BF16),
             pltpu.VMEM((5, 10, LOADS, 128), F32),
             pltpu.VMEM((5, 10, LOADS, 128), F32),
@@ -558,10 +642,12 @@
             pltpu.VMEM((4, NSUB // 2, 8, 128), F32),
             pltpu.VMEM((32, 128), F32),
             pltpu.VMEM((12, LOADS, 128), jnp.int32),
+            pltpu.VMEM((8, 128), jnp.int32),
             pltpu.VMEM((32, WIDE), F32),
             pltpu.VMEM((32, WIDE), F32),
             pltpu.VMEM((32, WIDE), F32),
-            pltpu.SemaphoreType.DMA((FACES,)),
+            pltpu.SemaphoreType.DMA((6,)),
+            pltpu.SemaphoreType.DMA((FACES + 1,)),
             pltpu.SemaphoreType.DMA((FACES,)),
             pltpu.SemaphoreType.DMA((NSEM,)),
             pltpu.SemaphoreType.DMA((NSEM,)),
@@ -569,7 +655,7 @@
         compiler_params=pltpu.CompilerParams(
             collective_id=0, has_side_effects=True, vmem_limit_bytes=48 * 1024 * 1024
         ),
-    )(fpad, inverse_h, schur_matrix, h_tail, coarse_inv, perm, cr, ids)
+    )(forces, h, schur, coarse_inv, perm, corner_rows, corner_ids, corner_count)
 
 
 def solution(mesh):

time: 130 us -> 98.5 us (0.76)
  Pallas kernels: 111 us -> 91.7 us
  local copies, waits for them, and re-layouts: 17 us -> 5.63 us
    pallas_call x1, Pallas kernels: 111 us -> 91.7 us  [body(): pl.pallas_call(kernel, out_shape=(out, out), in_specs=[hbm] * 8, out_spec...]
    unnamed x9 -> x14, local copies, waits for them, and re-layouts: 14.9 us -> 5.63 us
where the time goes in v2:
time: 98.5 us; the launch traced here: 98 us
  Pallas kernels  91.7 us (93%)
  local copies, waits for them, and re-layouts  5.63 us (6%)
    pallas_call x1, Pallas kernels, body(): pl.pallas_call(kernel, out_shape=(out, out), in_specs=[hbm] * 8, out_spec...  91.7 us
    unnamed x14, local copies, waits for them, and re-layouts  5.63 us

profile of v2, /device:TPU:1, one launch (start us, length us, event | category | flops | bytes accessed | tf_op | source)
XLA Modules:
  0.0 98.0 jit_solution(3162636686967119825)
XLA Ops:
  0.6 0.0 copy-start
  0.6 0.9 copy-done
  1.5 0.0 copy-start.1
  1.5 0.8 copy-done.1
  2.3 0.0 copy-start.2
  2.3 0.7 copy-done.2
  3.0 0.0 copy-start.3
  3.0 0.7 copy-done.3
  3.7 0.0 copy-start.4
  3.7 0.7 copy-done.4
  4.3 0.0 copy-start.5
  4.3 0.7 copy-done.5
  5.0 91.7 %shard_map.95 = (f32[2,16,650]{2,1,0:T(8,128)S(1)}, f32[2,16,650]{2,1,0:T(8,128)S(1)}) custom-call(f32[2,16,650]{2,1,0:T(8,128)S(1)} %copy-done, bf16[650,2,2600]{2,1,0:T(2,128)(2,1)} %bitcast.4, bf16[650,2,2600]{2,1,0:T(2,128)(2,1)} %bitcast.5, f32[8,1024]{1,0:T(8,128)S(1)} %copy-done.1, s32[6,2,96]{2,1,0:T(2,128)S(1)} %bitcast.3, s32[2,24]{1,0:T(2,128)S(1)} %copy-done.3, ...), custom_call_target="tpu_custom_call" | custom-call | tf_op jit(solution)/shard_map/pallas_call | solution.py:606
  96.7 0.6 copy.12
  97.4 0.6 copy.13
Async XLA Ops:
  0.6 0.9 copy-start
  1.5 0.8 copy-start.1
  2.3 0.7 copy-start.2
  3.0 0.7 copy-start.3
  3.7 0.7 copy-start.4
  4.3 0.7 copy-start.5

commit v3 on v2

--- a/solution.py
+++ b/solution.py
@@ -118,6 +118,14 @@
     def dev(x, z, c):
         return (x * 4 + z) * 2 + c
 
+    def away(i):
+        return (1 - i // 2) * (2 + i) + (i // 2) * (3 - i)
+
+    def peer(k):
+        x = lax.rem(xc + away(k // 8), 4)
+        z = lax.rem(zc + away(lax.rem(k // 2, 4)), 4)
+        return dev(x, z, lax.rem(core + 1 + lax.rem(k, 2), 2))
+
     def load(src, dst, sem, f):
         size = FACEQ if f < FACES else BLOCK - FACES * FACEQ
         rows = pl.ds(FACEQ * f, size)
@@ -137,11 +145,9 @@
 
     barrier = pltpu.get_barrier_semaphore()
 
-    @pl.loop(1, NSUB)
+    @pl.loop(0, NSUB - 1)
     def _(k):
-        pl.semaphore_signal(
-            barrier, inc=1, device_id=(lax.rem(g + k, NSUB), q), device_id_type=MESH
-        )
+        pl.semaphore_signal(barrier, inc=1, device_id=(peer(k), q), device_id_type=MESH)
 
     other = g + 1 - 2 * core
     for k in range(1, NROW):
@@ -185,15 +191,18 @@
 
     rows = slot_row(corner_rows, 24, 24).astype(F32)
     spot = jnp.broadcast_to(rows[0:1, :], (128, 128)).T[:SLOTS].astype(jnp.int32)
+    lane24 = lanes((24, 128))
     lane48 = lanes((SLOTS, 128))
-    upper = lax.broadcasted_iota(jnp.int32, (SLOTS, 128), 0) < 24
+    rest = jnp.zeros((8, 128), F32)
     for t in range(KFULL // 128):
-        hit = jnp.where(lane48 + 128 * t == spot, 1.0, 0.0)
-        oh[0, :, 128 * t : 128 * t + 128] = jnp.where(upper, hit, 0.0).astype(BF16)
-        oh[1, :, 128 * t : 128 * t + 128] = jnp.where(upper, 0.0, hit).astype(BF16)
+        for s in range(2):
+            hit = jnp.where(lane24 + 128 * t == spot[24 * s : 24 * s + 24], 1.0, 0.0)
+            oh[s, :, 128 * t : 128 * t + 128] = jnp.concatenate([hit, rest], axis=0).astype(BF16)
     for s in range(2):
         for f in range(FACES):
-            hv[s, 128 * f + FACEQ : 128 * f + 128, :] = jnp.zeros((32, NS), BF16)
+            hv[s, 128 * f + FACEQ : 128 * f + 128, :] = jnp.zeros((32, KFULL), BF16)
+        hv[s, :, KMAIN:] = jnp.zeros((WIDE, KFULL - KMAIN), BF16)
+        ht[s, :, KMAIN:] = jnp.zeros((128, KFULL - KMAIN), BF16)
     hco[...] = jnp.zeros((128, WIDE), BF16)
 
     def split(raw, start, dst, at, count):
@@ -201,7 +210,7 @@
         def _(i):
             pair = jnp.swapaxes(raw[pl.ds(start + 16 * i, 16)], 0, 1)
             for s in range(2):
-                dst[s, pl.ds(pl.multiple_of(at + 16 * i, 16), 16), :] = pair[s]
+                dst[s, pl.ds(pl.multiple_of(at + 16 * i, 16), 16), :NS] = pair[s]
 
     for f in range(FACES):
         load(h_hbm, raw_h, h_sem, f).wait()
@@ -212,9 +221,9 @@
     pl.semaphore_wait(barrier, NSUB - 1 + 2 * (NROW - 1))
 
     def to_plane(src_of, dst, sem):
-        @pl.loop(1, NSUB)
+        @pl.loop(0, NSUB - 1)
         def _(k):
-            far = lax.rem(g + k, NSUB)
+            far = peer(k)
             pltpu.make_async_remote_copy(
                 src_ref=src_of(far),
                 dst_ref=dst,
@@ -225,7 +234,7 @@
             ).start()
 
     def to_row(ref, sem):
-        for k in range(1, NROW):
+        for k in (2, 1, 3):
             pltpu.make_async_remote_copy(
                 src_ref=ref,
                 dst_ref=ref,
@@ -244,18 +253,14 @@
     to_plane(lambda far: ib.at[g], ib.at[g], IDS)
     to_row(fb.at[q], FORCES)
 
-    corner_h = jnp.zeros((SLOTS, WIDE), F32)
-    corner_t = jnp.zeros((SLOTS, 128), F32)
-    for s in range(2):
-        corner_h = corner_h + dot_nt(oh[s, :, :KMAIN], hv[s, :, :KMAIN])
-        corner_h = corner_h + dot_nt(oh[s, :, KMAIN:NS], hv[s, :, KMAIN:NS])
-        corner_t = corner_t + dot_nt(oh[s, :, :KMAIN], ht[s, :, :KMAIN])
-        corner_t = corner_t + dot_nt(oh[s, :, KMAIN:NS], ht[s, :, KMAIN:NS])
+    corner_h = jnp.concatenate([dot_nt(oh[s], hv[s])[:24] for s in range(2)], axis=0)
+    corner_t = jnp.concatenate([dot_nt(oh[s], ht[s])[:24] for s in range(2)], axis=0)
     corner_t = jnp.where(lane48 < BLOCK - FACES * FACEQ, corner_t, 0.0)
     hco[:SLOTS, :] = corner_h.astype(BF16)
     pieces = [corner_h[:, 128 * f : 128 * f + 128] for f in range(FACES)] + [corner_t]
     for t, tile in enumerate(pack_tiles(pieces, shift, 6)):
         hcb[q, :, 128 * t : 128 * t + 128] = tile.astype(BF16)
+
     to_row(hcb.at[q], HCORN)
 
     arrived(ib.at[pl.ds(0, NSUB - 1)], IDS)
@@ -272,9 +277,9 @@
 
     ca[g] = pick_columns(g)
 
-    @pl.loop(1, NSUB)
+    @pl.loop(0, NSUB - 1)
     def _(k):
-        far = lax.rem(g + k, NSUB)
+        far = peer(k)
         tb[far] = pick_columns(far)
         pltpu.make_async_remote_copy(
             src_ref=tb.at[far],
@@ -330,9 +335,7 @@
     to_row(cat.at[q], CFULL)
 
     for s in range(2):
-        rv[LOADS * s : LOADS * s + LOADS, :] = dot_nt(
-            xf[LOADS * s : LOADS * s + LOADS, :KMAIN], hv[s, :, :KMAIN]
-        ) + dot_nt(xf[LOADS * s : LOADS * s + LOADS, KMAIN:NS], hv[s, :, KMAIN:NS])
+        rv[LOADS * s : LOADS * s + LOADS, :] = dot_nt(xf[LOADS * s : LOADS * s + LOADS, :], hv[s])
 
     for f in range(FACES):
         for t in range(2):
@@ -473,7 +476,7 @@
         ra[n, chip_pos] = (
             plain[:8] + pltpu.roll(plain[8:], 16, 1) + pltpu.roll(sym[:8], 32, 1) + pltpu.roll(sym[8:], 48, 1)
         )
-        for k in range(1, 2 * NROW):
+        for k in (2, 6, 1, 3, 5, 7, 4):
             pos = lax.rem(chip_pos + k, 2 * NROW)
             pltpu.make_async_remote_copy(
                 src_ref=ra.at[n, chip_pos],
@@ -493,9 +496,9 @@
         arrived(ra.at[n, pl.ds(0, 2 * NROW - 1)], ARA + n)
         rb[n, chip_id] = tree([ra[n, i] for i in range(2 * NROW)])
 
-        @pl.loop(1, NSUB // 2)
+        @pl.loop(0, NSUB // 2 - 1)
         def _(k):
-            far = lax.rem(chip_id + k, NSUB // 2)
+            far = lax.rem(xc + away(k // 4), 4) * 4 + lax.rem(zc + away(lax.rem(k, 4)), 4)
             pltpu.make_async_remote_copy(
                 src_ref=rb.at[n, chip_id],
                 dst_ref=rb.at[n, chip_id],
@@ -617,9 +620,9 @@
             pltpu.SMEM((2,), jnp.int32),
             pltpu.VMEM((656, 2, NS), BF16),
             pltpu.VMEM((FACES * FACEQ, 2, NS), BF16),
+            pltpu.VMEM((2, WIDE, KFULL), BF16),
             pltpu.VMEM((2, WIDE, NS), BF16),
-            pltpu.VMEM((2, WIDE, NS), BF16),
-            pltpu.VMEM((2, 128, NS), BF16),
+            pltpu.VMEM((2, 128, KFULL), BF16),
             pltpu.VMEM((NSUB, 8, 128), jnp.int32),
             pltpu.VMEM((NSUB, 8, 128), F32),
             pltpu.VMEM((NSUB, 8, 128), F32),
@@ -628,7 +631,7 @@
             pltpu.VMEM((NROW, 32, SPILL), BF16),
             pltpu.VMEM((32, 128), F32),
             pltpu.VMEM((32, KFULL), BF16),
-            pltpu.VMEM((2, SLOTS, KFULL), BF16),
+            pltpu.VMEM((2, 32, KFULL), BF16),
             pltpu.VMEM((128, WIDE), BF16),
             pltpu.VMEM((NROW, SLOTS, SPILL), BF16),
             pltpu.VMEM((128, KFULL), BF16),
@@ -653,7 +656,7 @@
             pltpu.SemaphoreType.DMA((NSEM,)),
         ],
         compiler_params=pltpu.CompilerParams(
-            collective_id=0, has_side_effects=True, vmem_limit_bytes=48 * 1024 * 1024
+            collective_id=0, has_side_effects=True, vmem_limit_bytes=65000 * 1024
         ),
     )(forces, h, schur, coarse_inv, perm, corner_rows, corner_ids, corner_count)
 

time: 98.5 us -> 95.8 us (0.973)
  local copies, waits for them, and re-layouts: 5.63 us -> 3.08 us
    unnamed x14 -> x2, local copies, waits for them, and re-layouts: 5.63 us -> 3.08 us
where the time goes in v3:
time: 95.8 us; the launch traced here: 95.6 us
  Pallas kernels  91.9 us (96%)
  local copies, waits for them, and re-layouts  3.08 us (3%)
    pallas_call x1, Pallas kernels, body(): pl.pallas_call(kernel, out_shape=(out, out), in_specs=[hbm] * 8, out_spec...  91.9 us
    unnamed x2, local copies, waits for them, and re-layouts  3.08 us

profile of v3, /device:TPU:1, one launch (start us, length us, event | category | flops | bytes accessed | tf_op | source)
XLA Modules:
  0.0 95.6 jit_solution(12089673932134972872)
XLA Ops:
  0.6 91.9 %shard_map.95 = (f32[2,16,650]{2,1,0:T(8,128)}, f32[2,16,650]{2,1,0:T(8,128)}) custom-call(f32[2,16,650]{2,1,0:T(8,128)} %forces_in.1, bf16[650,2,2600]{2,1,0:T(2,128)(2,1)} %bitcast.3, bf16[650,2,2600]{2,1,0:T(2,128)(2,1)} %bitcast.4, f32[8,1024]{1,0:T(8,128)} %c_in.1, s32[6,2,96]{2,1,0:T(2,128)} %bitcast.5, s32[2,24]{1,0:T(2,128)} %rows_in.1, ...), custom_call_target="tpu_custom_call" | custom-call | tf_op jit(solution)/shard_map/pallas_call | solution.py:609
  92.5 1.5 %copy.12 = f32[2,16,650]{2,1,0:T(8,128)} copy(f32[2,16,650]{2,1,0:T(8,128)} %get-tuple-element.4) | data formatting | bytes 166400
  94.1 1.5 %copy.13 = f32[2,16,650]{2,1,0:T(8,128)} copy(f32[2,16,650]{2,1,0:T(8,128)} %get-tuple-element.5) | data formatting | bytes 166400

commit v4 on v3

--- a/solution.py
+++ b/solution.py
@@ -245,6 +245,11 @@
             ).start()
 
     drains = []
+
+    def drain():
+        while drains:
+            ref, sem = drains.pop()
+            pltpu.make_async_copy(ref, ref, send.at[sem]).wait()
 
     def arrived(ref, sem):
         pltpu.make_async_copy(ref, ref, recv.at[sem]).wait()
@@ -578,6 +583,7 @@
     v = corner_finish(2, flex)
     inner_start(3, dv[...], v)
     jump_send(4, v)
+    drain()
     inner_middle(3)
     image = jump_finish(4, v)
     unused, curvature = inner_finish(3)
@@ -593,8 +599,7 @@
     put_out(mult_out, mv[...] + combine(dv[...], step))
     put_out(res_out, rv[...] - combine(image, step))
 
-    for ref, sem in drains:
-        pltpu.make_async_copy(ref, ref, send.at[sem]).wait()
+    drain()
 
 
 def body(

time: 95.8 us -> 95.7 us (level)
  no operation moved by 1% of the time
where the time goes in v4:
time: 95.7 us; the launch traced here: 95.6 us
  Pallas kernels  91.8 us (96%)
  local copies, waits for them, and re-layouts  3.08 us (3%)
    pallas_call x1, Pallas kernels, body(): pl.pallas_call(kernel, out_shape=(out, out), in_specs=[hbm] * 8, out_spec...  91.8 us
    unnamed x2, local copies, waits for them, and re-layouts  3.08 us

profile of v4, /device:TPU:1, one launch (start us, length us, event | category | flops | bytes accessed | tf_op | source)
XLA Modules:
  0.0 95.6 jit_solution(9087228146435823614)
XLA Ops:
  0.6 91.8 %shard_map.95 = (f32[2,16,650]{2,1,0:T(8,128)}, f32[2,16,650]{2,1,0:T(8,128)}) custom-call(f32[2,16,650]{2,1,0:T(8,128)} %forces_in.1, bf16[650,2,2600]{2,1,0:T(2,128)(2,1)} %bitcast.3, bf16[650,2,2600]{2,1,0:T(2,128)(2,1)} %bitcast.4, f32[8,1024]{1,0:T(8,128)} %c_in.1, s32[6,2,96]{2,1,0:T(2,128)} %bitcast.5, s32[2,24]{1,0:T(2,128)} %rows_in.1, ...), custom_call_target="tpu_custom_call" | custom-call | tf_op jit(solution)/shard_map/pallas_call | solution.py:614
  92.5 1.5 %copy.12 = f32[2,16,650]{2,1,0:T(8,128)} copy(f32[2,16,650]{2,1,0:T(8,128)} %get-tuple-element.4) | data formatting | bytes 166400
  94.0 1.5 %copy.13 = f32[2,16,650]{2,1,0:T(8,128)} copy(f32[2,16,650]{2,1,0:T(8,128)} %get-tuple-element.5) | data formatting | bytes 166400
